TPU v7x, 256 devices: a whole 4x4x8 slice. The times are simulated.
256 devices in a mesh: batch: 16 (over z, core), seq: 16 (over y, x).
Axes of the slice: x: 4, y: 4, z: 8, core: 2. Of those that a mesh axis runs over, the one named last changes fastest.
Arguments:
- tokens: bfloat16 [16, 16384, 1408], P('batch', 'seq'), may hold values from -24 to 24
- w_qkv: bfloat16 [1408, 4224], P(None, 'seq'), may hold values from -0.170450765 to 0.170450765
- vis_index: int32 [16, 2560], P('batch', 'seq'), may hold values from 0 to 1023, as said below
- counts: int32 [16, 16], P('batch'), may hold values from 96 to 160, as said below
- d_out: bfloat16 [16, 2560, 1408], P('batch', 'seq'), may hold values from -6 to 6
Outputs:
- attn_out: bfloat16 [16, 2560, 1408], P('batch', 'seq')
- d_tokens: bfloat16 [16, 16384, 1408], P('batch', 'seq')
- d_wqkv: float32 [1408, 4224], P(None, 'seq')
Inputs may be any that keep to these rules, and one draw needn't show every extreme that they name: For every clip the 16 counts add up to exactly 2048, and some position block of every clip holds exactly 160. `vis_index`: within one position block's 160 entries all values differ; entry r names a visible tubelet when r is below that block's count and is ignored otherwise.
All inputs are finite; a program needn't handle non-finite values.
Results may differ from a plain program's by a relative error of at most 0.04.
Values may be sent and summed in bfloat16 or wider, within the bound.
A program may use at most 128 MiB of HBM per device.

v0:
```python
import jax
import jax.numpy as jnp
from jax import lax
from jax.sharding import PartitionSpec as P

HEAD = 88


EPSILON = 1e-06
MASKED = -1e30


def contract(left, right, left_dim, right_dim):
    return lax.dot_general(
        left, right, (((left_dim,), (right_dim,)), ((), ())), preferred_element_type=jnp.float32
    )


def head_pass(queries, key_rows, values, gradient, key_bias, block):
    inv_scale = HEAD ** (-0.5)
    length = queries.shape[0]
    head_width = queries.shape[1]
    blocks = length // block

    def block_step(running, block_in):
        acc_key, acc_value = running
        q_block, g_block = block_in
        scores = contract(q_block, key_rows, 1, 1) * inv_scale + key_bias[None, :]
        row_peak = jnp.max(scores, axis=1, keepdims=True)
        weights = jnp.exp(scores - row_peak)
        probs = weights / jnp.sum(weights, axis=1, keepdims=True)
        probs_low = probs.astype(jnp.bfloat16)
        attended = jnp.dot(probs_low, values, preferred_element_type=jnp.float32).astype(
            jnp.bfloat16
        )
        d_probs = contract(g_block, values, 1, 1)
        row_delta = jnp.sum(
            g_block.astype(jnp.float32) * attended.astype(jnp.float32), axis=1, keepdims=True
        )
        d_scores = (probs * (d_probs - row_delta) * inv_scale).astype(jnp.bfloat16)
        d_query = jnp.dot(d_scores, key_rows, preferred_element_type=jnp.float32).astype(
            jnp.bfloat16
        )
        acc_key = acc_key + contract(d_scores, q_block, 0, 0)
        acc_value = acc_value + contract(probs_low, g_block, 0, 0)
        return ((acc_key, acc_value), (attended, d_query))

    initial = (
        jnp.zeros((length, head_width), jnp.float32),
        jnp.zeros((length, head_width), jnp.float32),
    )
    (acc_key, acc_value), (attended, d_query) = lax.scan(
        block_step,
        initial,
        (queries.reshape(blocks, block, head_width), gradient.reshape(blocks, block, head_width)),
    )
    d_parts = jnp.stack(
        [
            d_query.reshape(length, head_width),
            acc_key.astype(jnp.bfloat16),
            acc_value.astype(jnp.bfloat16),
        ]
    )
    return (attended.reshape(length, head_width), d_parts)


def per_device(tokens, w_qkv, vis_index, counts, d_out):
    shards = lax.axis_size("seq")
    shard_here = lax.axis_index("seq")
    local_tokens = tokens[0]
    index_row = vis_index[0]
    count_row = counts[0]
    capacity = index_row.shape[0]
    model_width = local_tokens.shape[1]
    heads_here = w_qkv.shape[1] // (3 * HEAD)
    slot_total = shards * capacity
    own_count = lax.dynamic_index_in_dim(count_row, shard_here, keepdims=False)
    row_live = (jnp.arange(capacity, dtype=jnp.int32) < own_count)[:, None]
    picked = jnp.take(local_tokens, index_row, axis=0).astype(jnp.float32)
    centred = picked - jnp.mean(picked, axis=1, keepdims=True)
    inv_std = lax.rsqrt(jnp.mean(centred * centred, axis=1, keepdims=True) + EPSILON)
    normed = centred * inv_std
    normed_low = jnp.where(row_live, normed, 0.0).astype(jnp.bfloat16)
    grad_local = jnp.where(row_live, d_out[0], jnp.zeros_like(d_out[0]))
    grad_heads = lax.all_to_all(grad_local, "seq", split_axis=1, concat_axis=0, tiled=True)
    everyone = lax.all_gather(normed_low, "seq", axis=0, tiled=True)
    projected = jnp.dot(everyone, w_qkv, preferred_element_type=jnp.float32).astype(jnp.bfloat16)
    projected = projected.reshape(slot_total, heads_here, 3, HEAD).transpose(1, 2, 0, 3)
    grad_split = grad_heads.reshape(slot_total, heads_here, HEAD).transpose(1, 0, 2)
    slot_order = jnp.arange(slot_total, dtype=jnp.int32)
    slot_owner = slot_order // capacity
    slot_live = slot_order % capacity < jnp.take(count_row, slot_owner)
    key_bias = jnp.where(slot_live, 0.0, MASKED).astype(jnp.float32)
    attended, d_parts = jax.vmap(
        lambda qq, kk, vv, gg: head_pass(qq, kk, vv, gg, key_bias, 4 * capacity)
    )(projected[:, 0], projected[:, 1], projected[:, 2], grad_split)
    attended_flat = attended.transpose(1, 0, 2).reshape(slot_total, heads_here * HEAD)
    out_rows = lax.all_to_all(attended_flat, "seq", split_axis=0, concat_axis=1, tiled=True)
    attn_out = jnp.where(row_live, out_rows, jnp.zeros_like(out_rows))[None]
    d_projected = d_parts.transpose(2, 0, 1, 3).reshape(slot_total, heads_here * 3 * HEAD)
    d_weight = contract(everyone, d_projected, 0, 0)
    d_wqkv = lax.psum(d_weight, "batch")
    d_normed = lax.psum_scatter(
        contract(d_projected, w_qkv, 1, 1), "seq", scatter_dimension=0, tiled=True
    )
    d_picked = inv_std * (
        d_normed
        - jnp.mean(d_normed, axis=1, keepdims=True)
        - normed * jnp.mean(d_normed * normed, axis=1, keepdims=True)
    )
    d_picked = jnp.where(row_live, d_picked, 0.0)
    d_tokens = (
        jnp.zeros((local_tokens.shape[0], model_width), jnp.float32).at[index_row].add(d_picked)
    )
    return (attn_out, d_tokens.astype(jnp.bfloat16)[None], d_wqkv)


def solution(mesh):
    placed = (
        P("batch", "seq", None),
        P(None, "seq"),
        P("batch", "seq"),
        P("batch", None),
        P("batch", "seq", None),
    )
    return jax.shard_map(
        per_device,
        mesh=mesh,
        in_specs=placed,
        out_specs=(P("batch", "seq", None), P("batch", "seq", None), P(None, "seq")),
        check_vma=False,
    )
```

profile of v0, /device:TPU:1, one launch (start us, length us, event | category | flops | bytes accessed | tf_op | source)
XLA Modules:
  0.0 435.3 jit_solution(8690490886937017223)
XLA Ops:
  8.1 2.0 fusion.60
  14.0 2.4 squeeze.33
  17.7 7.6 %all-to-all-start = ((bf16[160,16,88]{2,0,1:T(8,128)(2,1)}), bf16[160,16,88]{2,0,1:T(8,128)(2,1)S(1)}, u32[]{:S(2)}, u32[]{:S(2)}) async-start(bf16[160,16,88]{2,0,1:T(8,128)(2,1)} %copy.28), calls=%async_computation | async-start | bytes 1310720 | tf_op jit(solution)/shard_map/all_to_all | solution.py:85
  26.2 4.3 fusion.58
  30.5 5.7 %fusion.57 = f32[2560]{0:T(1024)S(1)} fusion(pred[2560]{0:T(1024)(128)(4,1)S(1)} %compare_reduce_fusion, pred[2560]{0:T(1024)(128)(4,1)S(1)} %compare_reduce_fusion.1, pred[2560]{0:T(1024)(128)(4,1)S(1)} %compare_reduce_fusion.2, pred[2560]{0:T(1024)(128)(4,1)S(1)} %compare_reduce_fusion.3, pred[2560]{0:T(1024)(128)(4,1)S(1)} %compare_reduce_fusion.4, ...), kind=kLoop, calls=%fused_computation.103 | loop fusion | flops 76800 | bytes 43556 | tf_op jit(solution)/shard_map/jit(_where)/select_n | solution.py:93
  38.1 53.0 %all-gather.2.cloned.1.call-done = bf16[2560,1408]{1,0:T(8,128)(2,1)} async-done(((bf16[160,1408]{1,0:T(8,128)(2,1)}), bf16[2560,1408]{1,0:T(8,128)(2,1)}) %all-gather.2.cloned.1.call-update) | async-done | bytes 7208976 | tf_op jit(solution)/shard_map/all_gather | solution.py:86
  91.1 6.4 %convolution_convert_fusion.1 = bf16[2560,264]{0,1:T(8,128)(2,1)} fusion(bf16[2560,1408]{1,0:T(8,128)(2,1)} %all-gather.2.cloned.1.call-done, bf16[1408,264]{0,1:T(8,128)(2,1)S(1)} %copy-done.5), kind=kOutput, calls=%fused_computation.38 | convolution fusion | flops 1903841280 | bytes 9304064 | tf_op jit(solution)/shard_map/dot_general | solution.py:87
  97.5 2.7 copy.27
  101.4 89.6 %while.17 = (s32[]{:T(128)}, f32[1,2560,88]{1,2,0:T(8,128)}, f32[1,2560,88]{1,2,0:T(8,128)}, bf16[4,1,640,88]{2,3,1,0:T(8,128)(2,1)}, bf16[4,1,640,88]{2,3,1,0:T...) while((s32[]{:T(128)}, f32[1,2560,88]{1,2,0:T(8,128)}, ...), condition=%wide.region_6.7_spmd.clone, body=%wide.region_2.0_spmd.clone.sunk | while | flops 1759240320 | bytes 121918224 | solution.py:52
  101.4 2.1 fusion.93
  104.9 2.0 fusion.95
  106.9 3.4 multiply_reduce_fusion.2
  110.3 4.4 %multiply_convert_fusion.2 = bf16[640,2560]{1,0:T(8,128)(2,1)} fusion(f32[640,2560]{1,0:T(8,128)S(1)} %fusion.95, f32[640]{0:T(1024)S(1)} %get-tuple-element.250, bf16[1,2560,88]{2,1,0:T(8,128)(2,1)} %get-tuple-element.285, bf16[4,1,640,88]{2,3,1,0:T(8,128)(2,1)} %get-tuple-element.284, s32[]{:T(128)} %get-tuple-element.264), kind=kOutput, calls=%fused_computation.2.clone.1 | convolution fusion | flops 294912000 | bytes 10601472 | tf_op jit(solution)/shard_map/vmap()/while/body/eval_jaxpr/dot_general | solution.py:14
  114.7 3.7 fusion.96
  118.4 1.8 fusion.98
  120.2 2.5 fusion.97
  123.4 2.1 fusion.93
  126.8 2.0 fusion.95
  128.8 3.4 multiply_reduce_fusion.2
  132.2 4.3 multiply_convert_fusion.2
  136.6 4.0 fusion.96
  140.6 1.8 fusion.98
  142.4 2.8 fusion.97
  145.9 2.1 fusion.93
  149.4 2.0 fusion.95
  151.3 3.4 multiply_reduce_fusion.2
  154.8 4.3 multiply_convert_fusion.2
  159.1 4.0 fusion.96
  163.2 1.8 fusion.98
  164.9 2.8 fusion.97
  168.5 2.1 fusion.93
  171.9 2.0 fusion.95
  173.9 3.4 multiply_reduce_fusion.2
  177.3 4.4 %multiply_convert_fusion.2 = bf16[640,2560]{1,0:T(8,128)(2,1)} fusion(f32[640,2560]{1,0:T(8,128)S(1)} %fusion.95, f32[640]{0:T(1024)S(1)} %get-tuple-element.250, bf16[1,2560,88]{2,1,0:T(8,128)(2,1)} %get-tuple-element.285, bf16[4,1,640,88]{2,3,1,0:T(8,128)(2,1)} %get-tuple-element.284, s32[]{:T(128)} %get-tuple-element.264), kind=kOutput, calls=%fused_computation.2.clone.1 | convolution fusion | flops 294912000 | bytes 10601472 | tf_op jit(solution)/shard_map/vmap()/while/body/eval_jaxpr/dot_general | solution.py:14
  181.7 4.0 fusion.96
  185.7 1.8 fusion.98
  187.5 2.8 fusion.97
  195.0 8.5 %fusion.61 = f32[2560,1408]{1,0:T(8,128)} fusion(bf16[2560,264]{0,1:T(8,128)(2,1)S(1)} %bitcast.128, bf16[1408,264]{0,1:T(8,128)(2,1)} %param.8), kind=kOutput, calls=%fused_computation.117 | convolution fusion | flops 1903165440 | bytes 16513024 | tf_op jit(solution)/shard_map/dot_general | solution.py:14
  203.5 2.1 copy.37
  205.6 5.0 %all-to-all-start.1 = ((bf16[16,160,88]{2,1,0:T(8,128)(2,1)}), bf16[16,160,88]{2,1,0:T(8,128)(2,1)S(1)}, u32[]{:S(2)}, u32[]{:S(2)}) async-start(bf16[16,160,88]{2,1,0:T(8,128)(2,1)} %bitcast.28), calls=%async_computation.1 | async-start | bytes 1310720 | tf_op jit(solution)/shard_map/all_to_all | solution.py:98
  210.9 6.4 %fusion.62 = f32[1408,264]{0,1:T(8,128)} fusion(bf16[2560,1408]{1,0:T(8,128)(2,1)} %all-gather.2.cloned.1.call-done, bf16[2560,264]{0,1:T(8,128)(2,1)S(1)} %bitcast.129), kind=kOutput, calls=%fused_computation.118 | convolution fusion | flops 1903165440 | bytes 10047488 | tf_op jit(solution)/shard_map/dot_general | solution.py:14
  217.3 6.6 %all-to-all-done.1 = bf16[16,160,88]{2,1,0:T(8,128)(2,1)S(1)} async-done(((bf16[16,160,88]{2,1,0:T(8,128)(2,1)}), bf16[16,160,88]{2,1,0:T(8,128)(2,1)S(1)}, u32[]{:S(2)}, u32[]{:S(2)}) %all-to-all-start.1) | async-done | bytes 450592 | tf_op jit(solution)/shard_map/all_to_all | solution.py:98
  225.8 85.9 %reduce-scatter.2.cloned.1.call-done = f32[160,1408]{1,0:T(8,128)} async-done(((f32[2560,1408]{1,0:T(8,128)}), f32[160,1408]{1,0:T(8,128)}) %reduce-scatter.2.cloned.1.call-update) | async-done | bytes 901136 | tf_op jit(solution)/shard_map/reduce_scatter | solution.py:103
  311.7 1.5 fusion.59
  313.3 6.1 %scatter_custom_fusion = f32[1024,1408]{1,0:T(8,128)} fusion(s32[160]{0:T(256)S(1)} %bitcast.134, f32[]{:T(128)} %constant.83.clone.1, f32[160,1408]{1,0:T(8,128)} %reduce-scatter.2.cloned.1.call-done, f32[160]{0:T(256)S(1)} %broadcast_multiply_fusion, f32[160]{0:T(256)S(1)} %broadcast_multiply_fusion.1, f32[160]{0:T(256)S(1)} %add_rsqrt_fusion, ...), kind=kCustom, calls=%fused_computation.40 | custom fusion | flops 2252800 | bytes 7124992 | tf_op jit(solution)/shard_map/scatter-add | solution.py:113
  319.3 4.5 %convert_bitcast_fusion = bf16[1,1024,1408]{2,1,0:T(8,128)(2,1)} fusion(f32[1024,1408]{1,0:T(8,128)} %scatter_custom_fusion), kind=kLoop, calls=%fused_computation.39 | loop fusion | flops 1441792 | bytes 8650752 | tf_op jit(solution)/shard_map/broadcast_in_dim | solution.py:115
  323.9 102.4 %all-reduce.2.cloned.1.call-done = f32[1408,264]{0,1:T(8,128)} async-done(((f32[1408,264]{0,1:T(8,128)}), f32[1408,264]{0,1:T(8,128)}) %all-reduce.2.cloned.1.call-update) | async-done | bytes 1486864 | tf_op jit(solution)/shard_map/psum | solution.py:102
  426.2 2.6 copy.57
  (101 shorter events, 24.5 us)
Async XLA Ops:
  7.2 4.2 copy-start
  7.2 83.9 %all-gather.2.cloned.1.call-start = ((), (), s32[]{:S(2)}) async-start(), calls=%async_computation.3 | async-start | bytes 7659520 | tf_op jit(solution)/shard_map/all_gather | solution.py:86
  12.4 78.7 %copy-start.5 = (bf16[1408,264]{0,1:T(8,128)(2,1)S(1)}, bf16[1408,264]{0,1:T(8,128)(2,1)}, u32[]{:S(2)}) copy-start(bf16[1408,264]{0,1:T(8,128)(2,1)} %param.8) | copy-start | bytes 2230276
  17.7 19.4 %all-to-all-start = ((bf16[160,16,88]{2,0,1:T(8,128)(2,1)}), bf16[160,16,88]{2,0,1:T(8,128)(2,1)S(1)}, u32[]{:S(2)}, u32[]{:S(2)}) async-start(bf16[160,16,88]{2,0,1:T(8,128)(2,1)} %copy.28), calls=%async_computation | async-start | bytes 1310720 | tf_op jit(solution)/shard_map/all_to_all | solution.py:85
  25.3 286.4 %reduce-scatter.2.cloned.1.call-start = ((), (), s32[]{:S(2)}) async-start(), calls=%async_computation.4 | async-start | bytes 15319040 | tf_op jit(solution)/shard_map/reduce_scatter | solution.py:103
  106.9 3.5 copy-start.2
  114.7 5.5 %slice-start = ((s8[6553600]{0:T(1024)(128)(4,1)}), s8[2359296]{0:T(1024)(128)(4,1)S(1)}, s32[]{:S(2)}) async-start(s8[6553600]{0:T(1024)(128)(4,1)} %bitcast.125), calls=%async_computation.6 | async-start | bytes 4718592 | tf_op jit(solution)/shard_map/vmap()/while
  114.7 3.8 copy-start.3
  114.7 5.5 %slice-start.1 = ((s8[6553600]{0:T(1024)(128)(4,1)}), s8[4194304]{0:T(1024)(128)(4,1)S(1)}, s32[]{:S(2)}) async-start(s8[6553600]{0:T(1024)(128)(4,1)} %bitcast.125), calls=%async_computation.7 | async-start | bytes 8388608 | tf_op jit(solution)/shard_map/vmap()/while
  118.4 4.3 copy-start.4
  128.8 3.5 copy-start.2
  136.6 5.8 %slice-start = ((s8[6553600]{0:T(1024)(128)(4,1)}), s8[2359296]{0:T(1024)(128)(4,1)S(1)}, s32[]{:S(2)}) async-start(s8[6553600]{0:T(1024)(128)(4,1)} %bitcast.125), calls=%async_computation.6 | async-start | bytes 4718592 | tf_op jit(solution)/shard_map/vmap()/while
  136.6 4.0 copy-start.3
  136.6 5.8 %slice-start.1 = ((s8[6553600]{0:T(1024)(128)(4,1)}), s8[4194304]{0:T(1024)(128)(4,1)S(1)}, s32[]{:S(2)}) async-start(s8[6553600]{0:T(1024)(128)(4,1)} %bitcast.125), calls=%async_computation.7 | async-start | bytes 8388608 | tf_op jit(solution)/shard_map/vmap()/while
  140.6 4.6 %copy-start.4 = (bf16[640,88]{0,1:T(8,128)(2,1)S(1)}, bf16[640,88]{0,1:T(8,128)(2,1)}, u32[]{:S(2)}) copy-start(bf16[640,88]{0,1:T(8,128)(2,1)} %get-tuple-element.251) | copy-start | bytes 337924 | tf_op jit(solution)/shard_map/vmap()/while
  151.3 3.5 copy-start.2
  159.1 5.8 %slice-start = ((s8[6553600]{0:T(1024)(128)(4,1)}), s8[2359296]{0:T(1024)(128)(4,1)S(1)}, s32[]{:S(2)}) async-start(s8[6553600]{0:T(1024)(128)(4,1)} %bitcast.125), calls=%async_computation.6 | async-start | bytes 4718592 | tf_op jit(solution)/shard_map/vmap()/while
  159.1 4.0 copy-start.3
  159.1 5.8 %slice-start.1 = ((s8[6553600]{0:T(1024)(128)(4,1)}), s8[4194304]{0:T(1024)(128)(4,1)S(1)}, s32[]{:S(2)}) async-start(s8[6553600]{0:T(1024)(128)(4,1)} %bitcast.125), calls=%async_computation.7 | async-start | bytes 8388608 | tf_op jit(solution)/shard_map/vmap()/while
  163.2 4.6 %copy-start.4 = (bf16[640,88]{0,1:T(8,128)(2,1)S(1)}, bf16[640,88]{0,1:T(8,128)(2,1)}, u32[]{:S(2)}) copy-start(bf16[640,88]{0,1:T(8,128)(2,1)} %get-tuple-element.251) | copy-start | bytes 337924 | tf_op jit(solution)/shard_map/vmap()/while
  173.9 3.5 copy-start.2
  181.7 5.8 %slice-start = ((s8[6553600]{0:T(1024)(128)(4,1)}), s8[2359296]{0:T(1024)(128)(4,1)S(1)}, s32[]{:S(2)}) async-start(s8[6553600]{0:T(1024)(128)(4,1)} %bitcast.125), calls=%async_computation.6 | async-start | bytes 4718592 | tf_op jit(solution)/shard_map/vmap()/while
  181.7 4.0 copy-start.3
  181.7 5.8 %slice-start.1 = ((s8[6553600]{0:T(1024)(128)(4,1)}), s8[4194304]{0:T(1024)(128)(4,1)S(1)}, s32[]{:S(2)}) async-start(s8[6553600]{0:T(1024)(128)(4,1)} %bitcast.125), calls=%async_computation.7 | async-start | bytes 8388608 | tf_op jit(solution)/shard_map/vmap()/while
  185.7 4.6 %copy-start.4 = (bf16[640,88]{0,1:T(8,128)(2,1)S(1)}, bf16[640,88]{0,1:T(8,128)(2,1)}, u32[]{:S(2)}) copy-start(bf16[640,88]{0,1:T(8,128)(2,1)} %get-tuple-element.251) | copy-start | bytes 337924 | tf_op jit(solution)/shard_map/vmap()/while
  205.6 18.3 %all-to-all-start.1 = ((bf16[16,160,88]{2,1,0:T(8,128)(2,1)}), bf16[16,160,88]{2,1,0:T(8,128)(2,1)S(1)}, u32[]{:S(2)}, u32[]{:S(2)}) async-start(bf16[16,160,88]{2,1,0:T(8,128)(2,1)} %bitcast.28), calls=%async_computation.1 | async-start | bytes 1310720 | tf_op jit(solution)/shard_map/all_to_all | solution.py:98
  210.6 215.6 %all-reduce.2.cloned.1.call-start = ((), (), s32[]{:S(2)}) async-start(), calls=%async_computation.5 | async-start | bytes 2973696 | tf_op jit(solution)/shard_map/psum | solution.py:102
  313.2 115.6 %copy-start.1 = (bf16[1,1024,1408]{2,1,0:T(8,128)(2,1)S(1)}, bf16[1,1024,1408]{2,1,0:T(8,128)(2,1)}, u32[]{:S(2)}) copy-start(bf16[1,1024,1408]{2,1,0:T(8,128)(2,1)} %param.7) | copy-start | bytes 8650756
Sparse Core Ops, SparseCore 0:
  14.1 76.9 all-gather.1
  203.7 108.0 reduce-scatter.1
  314.8 111.3 all-reduce.1
where the time goes:
time: 437 us; the launch traced here: 435 us
  waiting for transfers between devices  249 us (57%)
  matrix products  94.7 us (22%)
  other arithmetic  43.8 us (10%)
  local copies, waits for them, and re-layouts  21 us (5%)
  between operations  13.9 us (3%)
  starting transfers between devices  12.9 us (3%)
    psum x1, waiting for transfers between devices, per_device(): d_wqkv = lax.psum(d_weight, 'batch')  102 us
    reduce_scatter x1, waiting for transfers between devices, per_device(): lax.psum_scatter(contract(d_projected, w_qkv, 1, 1), 'seq', scatter_dimen...  85.9 us
    dot_general x18, matrix products, contract(): lax.dot_general(left, right, (((left_dim,), (right_dim,)), ((), ())), pre...  67.5 us
    all_gather x1, waiting for transfers between devices, per_device(): everyone = lax.all_gather(normed_low, 'seq', axis=0, tiled=True)  53 us
    dot_general x4, matrix products, block_step(): jnp.dot(probs_low, values, preferred_element_type=jnp.float32)  13.8 us
  transfers between devices with their start and end apart: 5, of which 5 were waited for; matrix products, arithmetic and copies ran while one was open for 9% of the time, Pallas kernels for 0%

commit v1 on v0

v1 whole, which is shorter than its diff:
```python
import jax
import jax.numpy as jnp
from jax import lax
from jax.experimental import pallas as pl
from jax.experimental.pallas import tpu as pltpu
from jax.sharding import PartitionSpec as P

D = 1408
HEAD = 88
HEADS = 16
CAP = 160
HALF = 80
SURE = 96
TAIL = CAP - SURE
LIVE = 2048
PACKED = LIVE - HEADS * SURE
LANES = 128
WIDE = 3 * LANES
SEQ = 16
SIDE = 4
DEPTH = 8
EPSILON = 1e-06
LOG2E = 1.4426950408889634
LN2 = 0.6931471805599453
SCALE = HEAD ** (-0.5)
MESH = pl.DeviceIdType.MESH
BF = jnp.bfloat16
F32 = jnp.float32
VMEM = pltpu.VMEM
VMEM_BYTES = 60 * 2**20


def dot(left, right, left_dim=1, right_dim=0):
    return lax.dot_general(
        left, right, (((left_dim,), (right_dim,)), ((), ())), preferred_element_type=F32
    )


def wrap(value, size):
    return lax.rem(value + 2 * size, size)


PART = {0: (0, 80), 1: (0, 48), -1: (48, 32)}
BLOCK = {"o": (0, 0), "m": (-1, 0), "p": (1, 0), "a": (2, 1), "b": (2, -1)}
KEYS = (
    [("P1", s) for s in (1, -1)]
    + [("P1f", s) for s in (1, -1)]
    + [("P2", j, s) for j in "ompab" for s in (1, -1)]
    + [("P2f", j, s) for j in "omp" for s in (1, -1)]
    + [("P2f", "a", 1), ("P2f", "b", -1)]
)
IDS = {key: at for at, key in enumerate(KEYS)}


class Tree:
    def __init__(self, me, way, blocks, send_sem, recv_sem):
        self.y, self.x, self.way = me // SIDE, lax.rem(me, SIDE), way
        self.blocks, self.send_sem, self.recv_sem = blocks, send_sem, recv_sem
        self.memo = {}

    def node(self, half, first, second):
        key = (half, first % SIDE, second % SIDE)
        if key not in self.memo:
            first, second = first * self.way, second * self.way
            dy, dx = (second, first) if half == 0 else (first, second)
            self.memo[key] = wrap(self.y + dy, SIDE) * SIDE + wrap(self.x + dx, SIDE)
        return self.memo[key]

    def describe(self, key):
        kind, sign = key[0], key[-1]
        if kind == "P1":
            return (0, 0), 0, 0, sign
        if kind == "P1f":
            return (-sign, 0), sign, 0, sign
        first, part = BLOCK[key[1]]
        if kind == "P2":
            return (first, 0), part, 1, sign
        return (first, -sign), sign, 1, sign

    def copy(self, half, key, receiver=False):
        (first, second), part, axis, sign = self.describe(key)
        if receiver:
            first, second = (first - sign, second) if axis == 0 else (first, second - sign)
        start, rows = PART[part]
        ref = self.blocks.at[self.node(half, first, second), pl.ds(half * HALF + start, rows)]
        to = self.node(half, sign, 0) if axis == 0 else self.node(half, 0, sign)
        return pltpu.make_async_remote_copy(
            src_ref=ref, dst_ref=ref,
            send_sem=self.send_sem.at[half, IDS[key]], recv_sem=self.recv_sem.at[half, IDS[key]],
            device_id={"seq": to}, device_id_type=MESH,
        )

    def start(self, *key):
        for half in (0, 1):
            self.copy(half, key).start()

    def arrive(self, *key):
        for half in (0, 1):
            self.copy(half, key, True).wait_recv()

    def first(self):
        for s in (1, -1):
            self.start("P1", s)
        for s in (1, -1):
            self.start("P2", "o", s)

    def rest(self, done):
        for s in (1, -1):
            self.arrive("P1", s)
            self.start("P1f", s)
        for s in (1, -1):
            self.start("P2", "m", s)
            self.start("P2", "p", s)
        done([(-1, 0), (1, 0)])
        for s in (1, -1):
            self.arrive("P2", "o", s)
            self.start("P2f", "o", s)
        for s in (1, -1):
            self.arrive("P1f", s)
            for t in (1, -1):
                self.start("P2", "a" if s == 1 else "b", t)
        done([(0, -1), (0, 1), (2, 0)])
        for j in ("m", "p"):
            for s in (1, -1):
                self.arrive("P2", j, s)
                self.start("P2f", j, s)
        done([(-1, -1), (-1, 1), (1, -1), (1, 1)])
        for j in ("a", "b"):
            for s in (1, -1):
                self.arrive("P2", j, s)
                if ("P2f", j, s) in IDS:
                    self.start("P2f", j, s)
        for s in (1, -1):
            self.arrive("P2f", "o", s)
        done([(2, -1), (2, 1), (0, 2)])
        for j in ("m", "p"):
            for s in (1, -1):
                self.arrive("P2f", j, s)
        self.arrive("P2f", "a", 1)
        self.arrive("P2f", "b", -1)
        done([(-1, 2), (1, 2), (2, 2)])

    def finish(self):
        for key in KEYS:
            for half in (0, 1):
                self.copy(half, key).wait_send()


def gather_kernel(
    tokens, index, w, d_out,
    everyone_out, qkv, g, normed_out, inv_out, w_rows,
    everyone, w3, g_send, ring_send, ring_recv, g_ssem, g_rsem, out_sem,
):
    me = lax.axis_index("seq")
    core = lax.rem(lax.axis_index("batch"), 2)
    barrier = pltpu.get_barrier_semaphore()
    for step in range(1, SEQ):
        pl.semaphore_signal(
            barrier, inc=1, device_id={"seq": lax.rem(me + step, SEQ)}, device_id_type=MESH
        )

    hot = (lax.broadcasted_iota(jnp.int32, (tokens.shape[1], CAP), 0) == index[...]).astype(BF)
    picked = dot(hot, tokens[0], 0, 0)
    centred = picked - jnp.mean(picked, axis=1, keepdims=True)
    inv_std = lax.rsqrt(jnp.mean(centred * centred, axis=1, keepdims=True) + EPSILON)
    normed = centred * inv_std
    everyone[me] = normed.astype(BF)
    pl.semaphore_wait(barrier, SEQ - 1)
    tree = Tree(me, 1 - 2 * core, everyone, ring_send, ring_recv)
    tree.first()

    normed_out[...] = normed
    inv_out[...] = jnp.broadcast_to(inv_std, inv_out.shape)
    g_send[...] = jnp.zeros_like(g_send)
    for head in range(HEADS):
        g_send[head, :, :HEAD] = d_out[0, :, head * HEAD:(head + 1) * HEAD]

    def g_copy(step):
        to = lax.rem(me + step, SEQ)
        return pltpu.make_async_remote_copy(
            src_ref=g_send.at[to], dst_ref=g.at[me],
            send_sem=g_ssem.at[step], recv_sem=g_rsem.at[step],
            device_id={"seq": to}, device_id_type=MESH,
        )

    def g_arrival(step):
        origin = lax.rem(me - step + SEQ, SEQ)
        return pltpu.make_async_remote_copy(
            src_ref=g_send.at[origin], dst_ref=g.at[origin],
            send_sem=g_ssem.at[step], recv_sem=g_rsem.at[step],
            device_id={"seq": origin}, device_id_type=MESH,
        )

    def g_start(step, carry):
        g_copy(step).start()
        return carry

    w3[...] = jnp.zeros_like(w3)
    for part in range(3):
        w3[:, part * LANES:part * LANES + HEAD] = w[:, part * HEAD:(part + 1) * HEAD]

    lane = lax.broadcasted_iota(jnp.int32, (1, WIDE), 1)
    column_scale = jnp.where(lane < LANES, SCALE * LOG2E, 1.0).astype(F32)

    def project(places):
        rows = [everyone[owner, pl.ds(HALF * half, HALF), :] for owner, half in places]
        result = (dot(jnp.concatenate(rows, axis=0), w3[...]) * column_scale).astype(BF)
        for at, (owner, half) in enumerate(places):
            qkv[owner, pl.ds(HALF * half, HALF), :] = result[at * HALF:(at + 1) * HALF]
            part = (owner, pl.ds(HALF * half, HALF))
            pltpu.make_async_copy(everyone.at[part], everyone_out.at[part], out_sem).start()

    def done(offsets):
        project([(tree.node(half, *offset), half) for half in (0, 1) for offset in offsets])

    done([(0, 0)])
    tree.rest(done)
    lax.fori_loop(1, SEQ, g_start, 0)
    g[me] = g_send[me]
    for part in range(3):
        w_rows[part] = w3[:, part * LANES:(part + 1) * LANES].T[:SURE]

    def g_wait(step, carry):
        g_copy(step).wait_send()
        g_arrival(step).wait_recv()
        return carry

    lax.fori_loop(1, SEQ, g_wait, 0)
    tree.finish()
    pltpu.make_async_copy(everyone, everyone_out, out_sem).wait()


def gather_call(tokens, index, w, d_out):
    vmem = pl.BlockSpec(memory_space=VMEM)
    return pl.pallas_call(
        gather_kernel,
        out_shape=(
            jax.ShapeDtypeStruct((SEQ, CAP, D), BF),
            jax.ShapeDtypeStruct((SEQ, CAP, WIDE), BF),
            jax.ShapeDtypeStruct((SEQ, CAP, LANES), BF),
            jax.ShapeDtypeStruct((CAP, D), F32),
            jax.ShapeDtypeStruct((CAP, LANES), F32),
            jax.ShapeDtypeStruct((3, SURE, D), BF),
        ),
        in_specs=[vmem] * 4,
        out_specs=(pl.BlockSpec(memory_space=pl.ANY),) + (vmem,) * 5,
        scratch_shapes=[
            VMEM((SEQ, CAP, D), BF),
            VMEM((D, WIDE), BF),
            VMEM((HEADS, CAP, LANES), BF),
            pltpu.SemaphoreType.DMA((2, len(KEYS))),
            pltpu.SemaphoreType.DMA((2, len(KEYS))),
            pltpu.SemaphoreType.DMA((SEQ,)),
            pltpu.SemaphoreType.DMA((SEQ,)),
            pltpu.SemaphoreType.DMA,
        ],
        compiler_params=pltpu.CompilerParams(
            collective_id=1, has_side_effects=True, vmem_limit_bytes=VMEM_BYTES
        ),
        name="gather_project",
    )(tokens, index, w, d_out)


QB = 256


def attend(q, kt, k, va, vat, g, att, dq, dkt, dvt, between):
    dkt[...] = jnp.zeros_like(dkt)
    dvt[...] = jnp.zeros_like(dvt)
    lane = lax.broadcasted_iota(jnp.int32, (QB, LANES), 1)

    def block(at, carry):
        between(at)
        rows = pl.ds(at * QB, QB)
        queries = q[rows]
        scores = dot(queries, kt[...])
        weights = jnp.exp2(scores - jnp.max(scores, axis=1, keepdims=True)).astype(BF)
        raw = dot(weights, va[...])
        inverse = 1.0 / raw[:, HEAD:HEAD + 1]
        out = jnp.where(lane < HEAD, raw * inverse, 0.0)
        att[rows] = out.astype(BF)
        scaled = (g[rows].astype(F32) * inverse).astype(BF)
        delta = jnp.sum(scaled.astype(F32) * out, axis=1, keepdims=True)
        high = delta.astype(BF).astype(F32)
        extended = jnp.where(lane == HEAD, -high, scaled.astype(F32))
        extended = jnp.where(lane == HEAD + 1, high - delta, extended).astype(BF)
        d_scores = weights * dot(extended, vat[...]).astype(BF)
        dq[rows] = (dot(d_scores, k[...]) * SCALE).astype(BF)
        dkt[...] += dot(queries, d_scores, 0, 0)
        dvt[...] += dot(scaled, weights, 0, 0)
        return carry

    lax.fori_loop(0, LIVE // QB, block, 0)


HALF_LANES = 768
SHARD = WIDE // DEPTH


def attend_kernel(
    everyone_in, qkv, g_in, rank, normed_in, inv_in, w_rows, index,
    attn_out, d_tokens, d_wqkv,
    everyone, q, k, v, g, kt, vt, att, dq, dkt, dvt,
    w_side, d_slots, att_send, att_recv, d_recv, part_send, part_recv,
    dwt, pair_send, pair_recv, z_send, z_recv, z_all, z_other,
    w_ssem, w_rsem, d_ssem, d_rsem, p_ssem, p_rsem, a_ssem, a_rsem, c_ssem, c_rsem, z_ssem, z_rsem,
    in_sem,
):
    me = lax.axis_index("seq")
    batch = lax.axis_index("batch")
    core, z = lax.rem(batch, 2), batch // 2
    y, x = me // SIDE, lax.rem(me, SIDE)
    place = (y, x)

    def peer(axis, step):
        if axis == 0:
            return wrap(y + step, SIDE) * SIDE + x
        return y * SIDE + wrap(x + step, SIDE)

    def above(step):
        return wrap(z + step, DEPTH) * 2 + core

    other = batch + 1 - 2 * core
    barrier = pltpu.get_barrier_semaphore()
    for step in range(1, SEQ):
        pl.semaphore_signal(
            barrier, inc=1, device_id={"seq": lax.rem(me + step, SEQ)}, device_id_type=MESH
        )
    for step in range(1, DEPTH):
        pl.semaphore_signal(
            barrier, inc=1, device_id={"batch": above(step)}, device_id_type=MESH
        )
    pl.semaphore_signal(barrier, inc=1, device_id={"batch": other}, device_id_type=MESH)

    fetch = pltpu.make_async_copy(everyone_in, everyone, in_sem)
    fetch.start()

    def w_own(axis, sign):
        return pltpu.make_async_remote_copy(
            src_ref=w_rows, dst_ref=w_side.at[axis, place[axis], :, pl.ds(0, SURE)],
            send_sem=w_ssem.at[axis, (1 - sign) // 2], recv_sem=w_rsem.at[axis, (1 - sign) // 2],
            device_id={"seq": peer(axis, sign)}, device_id_type=MESH,
        )

    def w_from(axis, sign):
        ref = w_side.at[axis, wrap(place[axis] - sign, SIDE), :, pl.ds(0, SURE)]
        return pltpu.make_async_remote_copy(
            src_ref=w_rows, dst_ref=ref,
            send_sem=w_ssem.at[axis, (1 - sign) // 2], recv_sem=w_rsem.at[axis, (1 - sign) // 2],
            device_id={"seq": peer(axis, -sign)}, device_id_type=MESH,
        )

    def w_onward(axis, sign, receiver=False):
        origin = wrap(place[axis] - (2 * sign if receiver else sign), SIDE)
        slot = 2 + (1 - sign) // 2
        ref = w_side.at[axis, origin, :, pl.ds(0 if sign == 1 else SURE // 2, SURE // 2)]
        return pltpu.make_async_remote_copy(
            src_ref=ref, dst_ref=ref,
            send_sem=w_ssem.at[axis, slot], recv_sem=w_rsem.at[axis, slot],
            device_id={"seq": peer(axis, sign)}, device_id_type=MESH,
        )

    pl.semaphore_wait(barrier, SEQ - 1 + DEPTH)
    for axis in (0, 1):
        for sign in (1, -1):
            w_own(axis, sign).start()

    hot = (lax.broadcasted_iota(jnp.int32, (PACKED, HEADS * TAIL), 0) == rank[...]).astype(BF)
    sure_rows = HEADS * SURE
    tail = dot(hot, qkv[:, SURE:, :].reshape(HEADS * TAIL, WIDE)).astype(BF)
    for part, ref in enumerate((q, k, v)):
        lanes = slice(part * LANES, (part + 1) * LANES)
        ref[:sure_rows] = qkv[:, :SURE, lanes].reshape(sure_rows, LANES)
        ref[sure_rows:] = tail[:, lanes]
    g[:sure_rows] = g_in[:, :SURE, :].reshape(sure_rows, LANES)
    g[sure_rows:] = dot(hot, g_in[:, SURE:, :].reshape(HEADS * TAIL, LANES)).astype(BF)
    lane = lax.broadcasted_iota(jnp.int32, (LIVE, LANES), 1)
    ones = (lane == HEAD) | (lane == HEAD + 1)
    v[...] = jnp.where(ones, 1.0, v[...].astype(F32)).astype(BF)
    kt[...] = k[...].T
    vt[...] = v[...].T

    w_side[:, :, :, SURE:, :] = jnp.zeros((2, SIDE, 3, LANES - SURE, D), BF)
    for axis in (0, 1):
        w_side[axis, place[axis], :, :SURE, :] = w_rows[...]

    def between(at):
        @pl.when(at == 4)
        def _():
            for axis in (0, 1):
                for sign in (1, -1):
                    w_from(axis, sign).wait_recv()
                    w_onward(axis, sign).start()

    attend(q, kt, k, v, vt, g, att, dq, dkt, dvt, between)

    dk = (dkt[...].T * LN2).astype(BF)
    dv = dvt[...].T.astype(BF)
    packed = jnp.concatenate(
        [dq[sure_rows:], dk[sure_rows:], dv[sure_rows:], att[sure_rows:]], axis=1
    )
    loose = dot(hot, packed, 0, 0).astype(BF).reshape(SIDE, SIDE, TAIL, 4 * LANES)
    for part, value in enumerate((dq[:sure_rows], dk[:sure_rows], dv[:sure_rows])):
        lanes = slice(part * LANES, (part + 1) * LANES)
        d_slots[:, :, :SURE, lanes] = value.reshape(SIDE, SIDE, SURE, LANES)
    d_slots[:, :, SURE:, :] = loose[..., :WIDE]
    att_send[:, :, :SURE, :] = att[:sure_rows].reshape(SIDE, SIDE, SURE, LANES)
    att_send[:, :, SURE:, :] = loose[..., WIDE:]

    def d_copy(axis, step):
        to = wrap(place[axis] + step, SIDE)
        if axis == 0:
            src = d_slots.at[to, :, pl.ds(0, HALF)]
        else:
            src = d_slots.at[:, to, pl.ds(HALF, HALF)]
        return pltpu.make_async_remote_copy(
            src_ref=src, dst_ref=d_recv.at[axis, place[axis]],
            send_sem=d_ssem.at[axis, step], recv_sem=d_rsem.at[axis, step],
            device_id={"seq": peer(axis, step)}, device_id_type=MESH,
        )

    def d_arrival(axis, step):
        ref = d_recv.at[axis, wrap(place[axis] - step, SIDE)]
        return pltpu.make_async_remote_copy(
            src_ref=ref, dst_ref=ref,
            send_sem=d_ssem.at[axis, step], recv_sem=d_rsem.at[axis, step],
            device_id={"seq": peer(axis, step)}, device_id_type=MESH,
        )

    for step in (2, 1, 3):
        for axis in (0, 1):
            d_copy(axis, step).start()
    d_recv[0, y] = d_slots[y, :, :HALF, :]
    d_recv[1, x] = d_slots[:, x, HALF:, :]

    def a_copy(step):
        to = lax.rem(me + step, SEQ)
        return pltpu.make_async_remote_copy(
            src_ref=att_send.at[to // SIDE, lax.rem(to, SIDE)], dst_ref=att_recv.at[me],
            send_sem=a_ssem.at[step], recv_sem=a_rsem.at[step],
            device_id={"seq": to}, device_id_type=MESH,
        )

    def a_arrival(step):
        ref = att_recv.at[lax.rem(me - step + SEQ, SEQ)]
        return pltpu.make_async_remote_copy(
            src_ref=ref, dst_ref=ref,
            send_sem=a_ssem.at[step], recv_sem=a_rsem.at[step],
            device_id={"seq": lax.rem(me - step + SEQ, SEQ)}, device_id_type=MESH,
        )

    def a_start(step, carry):
        a_copy(step).start()
        return carry

    lax.fori_loop(1, SEQ, a_start, 0)
    att_recv[me] = att_send[y, x]

    fetch.wait()
    for first, last in ((0, 512), (512, 1024), (1024, D)):
        dwt[:, first:last] = dot(
            d_slots[...].reshape(SEQ * CAP, WIDE),
            everyone[:, :, first:last].reshape(SEQ * CAP, last - first), 0, 0,
        )

    def lanes_of(which):
        return pl.ds(pl.multiple_of(which * (D - HALF_LANES), LANES), HALF_LANES)

    pair_send[...] = dwt[:, lanes_of(1 - core)].astype(BF)

    def c_copy(slot, src, dst):
        return pltpu.make_async_remote_copy(
            src_ref=src, dst_ref=dst, send_sem=c_ssem.at[slot], recv_sem=c_rsem.at[slot],
            device_id={"batch": other}, device_id_type=MESH,
        )

    pair_copy = c_copy(0, pair_send, pair_recv)
    pair_copy.start()

    def p_copy(axis, step):
        return pltpu.make_async_remote_copy(
            src_ref=part_send.at[axis, wrap(place[axis] + step, SIDE)],
            dst_ref=part_recv.at[axis, place[axis]],
            send_sem=p_ssem.at[axis, step], recv_sem=p_rsem.at[axis, step],
            device_id={"seq": peer(axis, step)}, device_id_type=MESH,
        )

    def p_arrival(axis, step):
        ref = part_recv.at[axis, wrap(place[axis] - step, SIDE)]
        return pltpu.make_async_remote_copy(
            src_ref=ref, dst_ref=ref,
            send_sem=p_ssem.at[axis, step], recv_sem=p_rsem.at[axis, step],
            device_id={"seq": peer(axis, step)}, device_id_type=MESH,
        )

    for axis in (0, 1):
        for sign in (1, -1):
            w_onward(axis, sign, True).wait_recv()
    for axis in (0, 1):
        for step in (1, 2, 3):
            d_arrival(axis, step).wait_recv()
        left = jnp.concatenate(
            [d_recv[axis, head].reshape(SIDE * HALF, WIDE) for head in range(SIDE)], axis=1
        )
        partial = dot(left, w_side[axis].reshape(SIDE * WIDE, D))
        part_send[1 - axis] = partial.astype(BF).reshape(SIDE, HALF, D)
        for step in (2, 1, 3):
            p_copy(1 - axis, step).start()
    for axis in (0, 1):
        part_recv[axis, place[axis]] = part_send[axis, place[axis]]

    pair_copy.wait()
    z_send[...] = (dwt[:, lanes_of(core)] + pair_recv[...].astype(F32)).astype(BF).reshape(
        DEPTH, SHARD, HALF_LANES
    )

    def z_copy(phase, step):
        to = wrap(z + step, DEPTH)
        return pltpu.make_async_remote_copy(
            src_ref=z_send.at[to] if phase == 0 else z_all.at[z],
            dst_ref=z_recv.at[z] if phase == 0 else z_all.at[z],
            send_sem=z_ssem.at[phase, step], recv_sem=z_rsem.at[phase, step],
            device_id={"batch": above(step)}, device_id_type=MESH,
        )

    def z_arrival(phase, step):
        ref = (z_recv if phase == 0 else z_all).at[wrap(z - step, DEPTH)]
        return pltpu.make_async_remote_copy(
            src_ref=ref, dst_ref=ref,
            send_sem=z_ssem.at[phase, step], recv_sem=z_rsem.at[phase, step],
            device_id={"batch": above(step)}, device_id_type=MESH,
        )

    for step in (4, 3, 5, 2, 6, 1, 7):
        z_copy(0, step).start()
    z_recv[z] = z_send[z]

    def a_wait(step, carry):
        a_copy(step).wait_send()
        a_arrival(step).wait_recv()
        return carry

    lax.fori_loop(1, SEQ, a_wait, 0)
    for head in range(HEADS):
        attn_out[0, :, head * HEAD:(head + 1) * HEAD] = att_recv[head, :, :HEAD]

    for step in range(1, DEPTH):
        z_arrival(0, step).wait_recv()
    total = z_recv[0].astype(F32)
    for at in range(1, DEPTH):
        total = total + z_recv[at].astype(F32)
    z_all[z] = total.astype(BF)
    for step in (4, 3, 5, 2, 6, 1, 7):
        z_copy(1, step).start()

    for axis in (0, 1):
        for step in (1, 2, 3):
            p_arrival(axis, step).wait_recv()
    halves = []
    for axis in (1, 0):
        value = part_recv[axis, 0].astype(F32)
        for at in range(1, SIDE):
            value = value + part_recv[axis, at].astype(F32)
        halves.append(value)
    d_normed = jnp.concatenate(halves, axis=0)
    normed = normed_in[...]
    d_picked = inv_in[:, :1] * (
        d_normed
        - jnp.mean(d_normed, axis=1, keepdims=True)
        - normed * jnp.mean(d_normed * normed, axis=1, keepdims=True)
    )
    spread = (lax.broadcasted_iota(jnp.int32, (d_tokens.shape[1], CAP), 0) == index[...]).astype(BF)
    d_tokens[0] = dot(spread, d_picked.astype(BF)).astype(BF)

    for step in range(1, DEPTH):
        z_arrival(1, step).wait_recv()
    last = c_copy(1, z_all, z_other)
    last.start()
    last.wait()
    mine, theirs = (
        ref[...].astype(F32).reshape(WIDE, HALF_LANES) for ref in (z_all, z_other)
    )
    low = jnp.where(core == 0, mine, theirs)
    high = jnp.where(core == 0, theirs, mine)
    overlap = 2 * HALF_LANES - D
    full = jnp.concatenate([low, high[:, overlap:]], axis=1)
    for part in range(3):
        d_wqkv[:, part * HEAD:(part + 1) * HEAD] = full[part * LANES:(part + 1) * LANES].T[:, :HEAD]

    for axis in (0, 1):
        for sign in (1, -1):
            w_own(axis, sign).wait_send()
            w_onward(axis, sign).wait_send()
        for step in (1, 2, 3):
            d_copy(axis, step).wait_send()
            p_copy(axis, step).wait_send()
    for step in range(1, DEPTH):
        z_copy(0, step).wait_send()
        z_copy(1, step).wait_send()


def attend_call(everyone, qkv, g, rank, normed, inv, w_rows, index, positions):
    vmem = pl.BlockSpec(memory_space=VMEM)
    dma = pltpu.SemaphoreType.DMA
    return pl.pallas_call(
        attend_kernel,
        out_shape=(
            jax.ShapeDtypeStruct((1, CAP, D), BF),
            jax.ShapeDtypeStruct((1, positions, D), BF),
            jax.ShapeDtypeStruct((D, 3 * HEAD), F32),
        ),
        in_specs=[pl.BlockSpec(memory_space=pl.ANY)] + [vmem] * 7,
        out_specs=(vmem,) * 3,
        scratch_shapes=[
            VMEM((SEQ, CAP, D), BF),
            VMEM((LIVE, LANES), BF),
            VMEM((LIVE, LANES), BF),
            VMEM((LIVE, LANES), BF),
            VMEM((LIVE, LANES), BF),
            VMEM((LANES, LIVE), BF),
            VMEM((LANES, LIVE), BF),
            VMEM((LIVE, LANES), BF),
            VMEM((LIVE, LANES), BF),
            VMEM((LANES, LIVE), F32),
            VMEM((LANES, LIVE), F32),
            VMEM((2, SIDE, 3, LANES, D), BF),
            VMEM((SIDE, SIDE, CAP, WIDE), BF),
            VMEM((SIDE, SIDE, CAP, LANES), BF),
            VMEM((SEQ, CAP, LANES), BF),
            VMEM((2, SIDE, SIDE, HALF, WIDE), BF),
            VMEM((2, SIDE, HALF, D), BF),
            VMEM((2, SIDE, HALF, D), BF),
            VMEM((WIDE, D), F32),
            VMEM((WIDE, HALF_LANES), BF),
            VMEM((WIDE, HALF_LANES), BF),
            VMEM((DEPTH, SHARD, HALF_LANES), BF),
            VMEM((DEPTH, SHARD, HALF_LANES), BF),
            VMEM((DEPTH, SHARD, HALF_LANES), BF),
            VMEM((DEPTH, SHARD, HALF_LANES), BF),
            dma((2, 4)), dma((2, 4)),
            dma((2, 4)), dma((2, 4)),
            dma((2, 4)), dma((2, 4)),
            dma((SEQ,)), dma((SEQ,)),
            dma((2,)), dma((2,)),
            dma((2, DEPTH)), dma((2, DEPTH)),
            dma,
        ],
        compiler_params=pltpu.CompilerParams(
            collective_id=2, has_side_effects=True, vmem_limit_bytes=VMEM_BYTES
        ),
        name="attend_backward",
    )(everyone, qkv, g, rank, normed, inv, w_rows, index)


def per_device(tokens, w_qkv, vis_index, counts, d_out):
    extra = counts[0] - SURE
    order = jnp.arange(SEQ, dtype=jnp.int32)
    before = jnp.sum(jnp.where(order[None, :] < order[:, None], extra[None, :], 0), axis=1)
    within = jnp.arange(TAIL, dtype=jnp.int32)
    rank = jnp.where(within[None, :] < extra[:, None], before[:, None] + within[None, :], -1)
    rank = rank.reshape(1, SEQ * TAIL).astype(jnp.int32)
    everyone, qkv, g, normed, inv, w_rows = gather_call(tokens, vis_index, w_qkv, d_out)
    return tuple(
        attend_call(everyone, qkv, g, rank, normed, inv, w_rows, vis_index, tokens.shape[1])
    )


def solution(mesh):
    placed = (
        P("batch", "seq", None),
        P(None, "seq"),
        P("batch", "seq"),
        P("batch", None),
        P("batch", "seq", None),
    )
    return jax.shard_map(
        per_device,
        mesh=mesh,
        in_specs=placed,
        out_specs=(P("batch", "seq", None), P("batch", "seq", None), P(None, "seq")),
        check_vma=False,
    )
```

time: 437 us -> 163 us (0.37)
  waiting for transfers between devices: 249 us -> 0 us
  Pallas kernels: 0 us -> 153 us
  matrix products: 94.7 us -> 0 us
  other arithmetic: 43.8 us -> 0.85 us
  between operations: 13.9 us -> 0.67 us
  starting transfers between devices: 12.9 us -> 0 us
  local copies, waits for them, and re-layouts: 21 us -> 8.25 us
    pallas_call x0 -> x2, Pallas kernels: none -> 153 us  [the longest x1 92.5 us: attend_call(): pl.pallas_call(attend_kernel, out_shape=(jax.ShapeDtypeStruct((1, CAP, D)...]
    psum x1 -> x0, waiting for transfers between devices: 102 us -> none  [per_device(): d_wqkv = lax.psum(d_weight, 'batch')]
    dot_general x27 -> x0, matrix products: 94.7 us -> none  [the longest x18 67.5 us: contract(): lax.dot_general(left, right, (((left_dim,), (right_dim,)), ((), ())), pre...]
    reduce_scatter x1 -> x0, waiting for transfers between devices: 85.9 us -> none  [per_device(): lax.psum_scatter(contract(d_projected, w_qkv, 1, 1), 'seq', scatter_dimen...]
    all_gather x1 -> x0, waiting for transfers between devices: 53 us -> none  [per_device(): everyone = lax.all_gather(normed_low, 'seq', axis=0, tiled=True)]
    all_to_all x2 -> x0, starting transfers between devices: 12.5 us -> none  [the longest x1 7.58 us: per_device(): lax.all_to_all(grad_local, 'seq', split_axis=1, concat_axis=0, tiled=True)]
    div x7 -> x0, other arithmetic: 7.82 us -> none  [the longest x4 7.8 us: block_step(): probs = weights / jnp.sum(weights, axis=1, keepdims=True)]
    reduce_sum x7 -> x1, other arithmetic: 7.69 us -> 0.12 us  [per_device(): jnp.sum(jnp.where(order[None, :] < order[:, None], extra[None, :], 0), ax...]
  transfers between devices with their start and end apart: 5 -> 0, of which waited for: 5 -> 0; matrix products, arithmetic and copies ran while one was open for 9% -> 0% of each run, Pallas kernels for 0% -> 0%
where the time goes in v1:
time: 163 us
  Pallas kernels  153 us (94%)
  local copies, waits for them, and re-layouts  8.25 us (5%)
    pallas_call x1, Pallas kernels, attend_call(): pl.pallas_call(attend_kernel, out_shape=(jax.ShapeDtypeStruct((1, CAP, D)...  92.5 us
    pallas_call x1, Pallas kernels, gather_call(): pl.pallas_call(gather_kernel, out_shape=(jax.ShapeDtypeStruct((SEQ, CAP,...  60.8 us
    unnamed x7, local copies, waits for them, and re-layouts  4.62 us

profile of v1, /device:TPU:1, one launch (start us, length us, event | category | flops | bytes accessed | tf_op | source)
XLA Modules:
  0.0 163.1 jit_solution(9835282862505172869)
XLA Ops:
  0.6 0.7 add_bitcast_fusion
  1.3 0.1 select_reduce_fusion
  1.4 0.1 add_select_fusion
  1.5 0.7 select_n.20.rank
  2.2 2.3 %copy.10.w = bf16[1408,264]{1,0:T(8,128)(2,1)} copy(bf16[1408,264]{0,1:T(8,128)(2,1)} %param.6) | data formatting | bytes 1486848 | tf_op args[1]
  4.4 60.8 %gather_project.1 = (bf16[16,160,1408]{2,1,0:T(8,128)(2,1)}, bf16[16,160,384]{2,1,0:T(8,128)(2,1)}, bf16[16,160,128]{2,1,0:T(8,128)(2,1)}, f32[160,1408]{1,0:T(8...) custom-call(bf16[1,1024,1408]{2,1,0:T(8,128)(2,1)} %tokens.1, s32[1,160]{1,0:T(1,128)} %index.3, ...), custom_call_target="tpu_custom_call" | custom-call | tf_op jit(solution)/shard_map/gather_project/pallas_call | solution.py:235
  65.3 92.5 %attend_backward.1 = (bf16[1,160,1408]{2,1,0:T(8,128)(2,1)}, bf16[1,1024,1408]{2,1,0:T(8,128)(2,1)}, f32[1408,264]{1,0:T(8,128)}) custom-call(bf16[16,160,1408]{2,1,0:T(8,128)(2,1)} %get-tuple-element.9.everyone_in, bf16[16,160,384]{2,1,0:T(8,128)(2,1)} %get-tuple-element.10.qkv, bf16[16,160,128]{2,1,0:T(8,128)(2,1)} %get-tuple-element.11.g_in, ...), custom_call_target="tpu_custom_call" | custom-call | tf_op jit(solution)/shard_map/attend_backward/pallas_call | solution.py:605
  157.8 0.0 copy-start.1
  157.8 0.0 copy-start
  157.8 3.0 %copy.11 = f32[1408,264]{0,1:T(8,128)} copy(f32[1408,264]{1,0:T(8,128)} %get-tuple-element.20) | data formatting | bytes 2973696 | tf_op jit(solution)/shard_map/attend_backward/pallas_call | solution.py:605
  160.8 0.0 copy-done.1
  160.8 0.8 copy.14
  161.5 0.0 copy-done
  161.5 1.6 copy.15
Async XLA Ops:
  157.8 3.0 %copy-start.1 = (bf16[1,160,1408]{2,1,0:T(8,128)(2,1)S(1)}, bf16[1,160,1408]{2,1,0:T(8,128)(2,1)}, u32[]{:S(2)}) copy-start(bf16[1,160,1408]{2,1,0:T(8,128)(2,1)} %get-tuple-element.24) | copy-start | bytes 1351684
  157.8 3.7 %copy-start = (bf16[1,1024,1408]{2,1,0:T(8,128)(2,1)S(1)}, bf16[1,1024,1408]{2,1,0:T(8,128)(2,1)}, u32[]{:S(2)}) copy-start(bf16[1,1024,1408]{2,1,0:T(8,128)(2,1)} %get-tuple-element.25) | copy-start | bytes 8650756

commit v2 on v1

v2 whole, which is shorter than its diff:
```python
import jax
import jax.numpy as jnp
from jax import lax
from jax.experimental import pallas as pl
from jax.experimental.pallas import tpu as pltpu
from jax.sharding import PartitionSpec as P

D = 1408
HEAD = 88
HEADS = 16
CAP = 160
HALF = 80
SURE = 96
TAIL = CAP - SURE
LIVE = 2048
PACKED = LIVE - HEADS * SURE
LANES = 128
WIDE = 3 * LANES
SEQ = 16
SIDE = 4
DEPTH = 8
EPSILON = 1e-06
LOG2E = 1.4426950408889634
LN2 = 0.6931471805599453
SCALE = HEAD ** (-0.5)
MESH = pl.DeviceIdType.MESH
BF = jnp.bfloat16
F32 = jnp.float32
VMEM = pltpu.VMEM
VMEM_BYTES = 62 * 2**20


def dot(left, right, left_dim=1, right_dim=0):
    return lax.dot_general(
        left, right, (((left_dim,), (right_dim,)), ((), ())), preferred_element_type=F32
    )


def wrap(value, size):
    return lax.rem(value + 2 * size, size)


PART = {0: (0, 80), 1: (0, 48), -1: (48, 32)}
BLOCK = {"o": (0, 0), "m": (-1, 0), "p": (1, 0), "a": (2, 1), "b": (2, -1)}
KEYS = (
    [("P1", s) for s in (1, -1)]
    + [("P1f", s) for s in (1, -1)]
    + [("P2", j, s) for j in "ompab" for s in (1, -1)]
    + [("P2f", j, s) for j in "omp" for s in (1, -1)]
    + [("P2f", "a", 1), ("P2f", "b", -1)]
)
IDS = {key: at for at, key in enumerate(KEYS)}


class Tree:
    def __init__(self, me, way, blocks, send_sem, recv_sem):
        self.y, self.x, self.way = me // SIDE, lax.rem(me, SIDE), way
        self.blocks, self.send_sem, self.recv_sem = blocks, send_sem, recv_sem
        self.memo = {}
        self.slots = {}
        for half in (0, 1):
            for first in range(SIDE):
                for second in range(SIDE):
                    self.slot(half, first, second)

    def node(self, half, first, second):
        key = (half, first % SIDE, second % SIDE)
        if key not in self.memo:
            first, second = first * self.way, second * self.way
            dy, dx = (second, first) if half == 0 else (first, second)
            self.memo[key] = wrap(self.y + dy, SIDE) * SIDE + wrap(self.x + dx, SIDE)
        return self.memo[key]

    def slot(self, half, first, second):
        key = (half, first % SIDE, second % SIDE)
        if key not in self.slots:
            node = self.node(half, first, second)
            self.slots[key] = node if half == 0 else lax.rem(node, SIDE) * SIDE + node // SIDE
        return self.slots[key]

    def describe(self, key):
        kind, sign = key[0], key[-1]
        if kind == "P1":
            return (0, 0), 0, 0, sign
        if kind == "P1f":
            return (-sign, 0), sign, 0, sign
        first, part = BLOCK[key[1]]
        if kind == "P2":
            return (first, 0), part, 1, sign
        return (first, -sign), sign, 1, sign

    def copy(self, half, key, receiver=False):
        (first, second), part, axis, sign = self.describe(key)
        if receiver:
            first, second = (first - sign, second) if axis == 0 else (first, second - sign)
        start, rows = PART[part]
        ref = self.blocks.at[half, self.slot(half, first, second), pl.ds(start, rows)]
        to = self.node(half, sign, 0) if axis == 0 else self.node(half, 0, sign)
        return pltpu.make_async_remote_copy(
            src_ref=ref, dst_ref=ref,
            send_sem=self.send_sem.at[half, IDS[key]], recv_sem=self.recv_sem.at[half, IDS[key]],
            device_id={"seq": to}, device_id_type=MESH,
        )

    def start(self, *key):
        for half in (0, 1):
            self.copy(half, key).start()

    def arrive(self, *key):
        for half in (0, 1):
            self.copy(half, key, True).wait_recv()

    def first(self):
        for s in (1, -1):
            self.start("P1", s)
        for s in (1, -1):
            self.start("P2", "o", s)

    def rest(self, done, late):
        for s in (1, -1):
            self.arrive("P1", s)
            self.start("P1f", s)
        for s in (1, -1):
            self.start("P2", "m", s)
            self.start("P2", "p", s)
        done([(-1, 0), (1, 0)])
        for s in (1, -1):
            self.arrive("P2", "o", s)
            self.start("P2f", "o", s)
        for s in (1, -1):
            self.arrive("P1f", s)
            for t in (1, -1):
                self.start("P2", "a" if s == 1 else "b", t)
        done([(0, -1), (0, 1), (2, 0)])
        for j in ("m", "p"):
            for s in (1, -1):
                self.arrive("P2", j, s)
                self.start("P2f", j, s)
        done([(-1, -1), (-1, 1), (1, -1), (1, 1)])
        for j in ("a", "b"):
            for s in (1, -1):
                self.arrive("P2", j, s)
                if ("P2f", j, s) in IDS:
                    self.start("P2f", j, s)
        late()
        for s in (1, -1):
            self.arrive("P2f", "o", s)
        done([(2, -1), (2, 1), (0, 2)])
        for j in ("m", "p"):
            for s in (1, -1):
                self.arrive("P2f", j, s)
        self.arrive("P2f", "a", 1)
        self.arrive("P2f", "b", -1)
        done([(-1, 2), (1, 2), (2, 2)])

    def finish(self):
        for key in KEYS:
            for half in (0, 1):
                self.copy(half, key).wait_send()


QB = 256


def attend(q, kt, k, va, vat, g, att, dq, dkt, dvt, between):
    dkt[...] = jnp.zeros_like(dkt)
    dvt[...] = jnp.zeros_like(dvt)
    lane = lax.broadcasted_iota(jnp.int32, (QB, LANES), 1)

    def block(at, carry):
        between(at)
        rows = pl.ds(at * QB, QB)
        queries = q[rows]
        scores = dot(queries, kt[...])
        weights = jnp.exp2(scores - jnp.max(scores, axis=1, keepdims=True)).astype(BF)
        raw = dot(weights, va[...])
        inverse = 1.0 / raw[:, HEAD:HEAD + 1]
        out = jnp.where(lane < HEAD, raw * inverse, 0.0)
        att[rows] = out.astype(BF)
        scaled = (g[rows].astype(F32) * inverse).astype(BF)
        delta = jnp.sum(scaled.astype(F32) * out, axis=1, keepdims=True)
        high = delta.astype(BF).astype(F32)
        extended = jnp.where(lane == HEAD, -high, scaled.astype(F32))
        extended = jnp.where(lane == HEAD + 1, high - delta, extended).astype(BF)
        d_scores = weights * dot(extended, vat[...]).astype(BF)
        dq[rows] = (dot(d_scores, k[...]) * SCALE).astype(BF)
        dkt[...] += dot(queries, d_scores, 0, 0)
        dvt[...] += dot(scaled, weights, 0, 0)
        return carry

    lax.fori_loop(0, LIVE // QB, block, 0)


HALF_LANES = 768
SHARD = WIDE // DEPTH
FIRST = SEQ * HALF
MORE = SURE - HALF
PACK_AT = FIRST + SEQ * MORE


def layer_kernel(
    tokens_in, w, d_out, rank, index,
    attn_out, d_tokens_out, d_wqkv,
    rows_buf, blocks, normed_buf, inv_buf, w_rows, w_side, w3, g_send, g_recv, qkv,
    q, k, v, g, kt, vt, att, dq, dkt, dvt,
    d_send, att_send, att_recv, d_recv, part_send, part_recv,
    dwt, pair_send, pair_recv, z_send, z_recv, z_all, z_other,
    t_ssem, t_rsem, g_ssem, g_rsem, w_ssem, w_rsem,
    d_ssem, d_rsem, p_ssem, p_rsem, a_ssem, a_rsem, c_ssem, c_rsem, z_ssem, z_rsem, o_ssem, o_rsem,
    in_sem, out_sem,
):
    me = lax.axis_index("seq")
    batch = lax.axis_index("batch")
    core, z = lax.rem(batch, 2), batch // 2
    y, x = me // SIDE, lax.rem(me, SIDE)
    place = (y, x)

    def peer(axis, step):
        if axis == 0:
            return wrap(y + step, SIDE) * SIDE + x
        return y * SIDE + wrap(x + step, SIDE)

    def above(step):
        return wrap(z + step, DEPTH) * 2 + core

    other = batch + 1 - 2 * core

    fetch = pltpu.make_async_copy(tokens_in.at[0], rows_buf, in_sem)
    fetch.start()
    barrier = pltpu.get_barrier_semaphore()
    for step in range(1, SEQ):
        pl.semaphore_signal(
            barrier, inc=1, device_id={"seq": lax.rem(me + step, SEQ)}, device_id_type=MESH
        )
    for step in range(1, DEPTH):
        pl.semaphore_signal(
            barrier, inc=1, device_id={"batch": above(step)}, device_id_type=MESH
        )
    pl.semaphore_signal(barrier, inc=1, device_id={"batch": other}, device_id_type=MESH)

    def remote(src, dst, sems, at, to, where="seq"):
        return pltpu.make_async_remote_copy(
            src_ref=src, dst_ref=dst, send_sem=sems[0].at[at], recv_sem=sems[1].at[at],
            device_id={where: to}, device_id_type=MESH,
        )

    w_sems = (w_ssem, w_rsem)

    def w_own(axis, sign):
        dst = w_side.at[axis, place[axis], :, pl.ds(0, SURE)]
        return remote(w_rows, dst, w_sems, (axis, (1 - sign) // 2), peer(axis, sign))

    def w_from(axis, sign):
        dst = w_side.at[axis, wrap(place[axis] - sign, SIDE), :, pl.ds(0, SURE)]
        return remote(w_rows, dst, w_sems, (axis, (1 - sign) // 2), peer(axis, -sign))

    def w_onward(axis, sign, receiver=False):
        origin = wrap(place[axis] - (2 * sign if receiver else sign), SIDE)
        ref = w_side.at[axis, origin, :, pl.ds(0 if sign == 1 else SURE // 2, SURE // 2)]
        return remote(ref, ref, w_sems, (axis, 2 + (1 - sign) // 2), peer(axis, sign))

    fetch.wait()
    spread = (lax.broadcasted_iota(jnp.int32, (rows_buf.shape[0], CAP), 0) == index[...]).astype(BF)
    picked = dot(spread, rows_buf[...], 0, 0)
    centred = picked - jnp.mean(picked, axis=1, keepdims=True)
    inv_std = lax.rsqrt(jnp.mean(centred * centred, axis=1, keepdims=True) + EPSILON)
    normed = centred * inv_std
    pl.semaphore_wait(barrier, SEQ - 1 + DEPTH)
    blocks[0, me] = normed[:HALF].astype(BF)
    blocks[1, x * SIDE + y] = normed[HALF:].astype(BF)
    tree = Tree(me, 1 - 2 * core, blocks, t_ssem, t_rsem)
    tree.first()
    normed_buf[...] = normed
    inv_buf[...] = jnp.broadcast_to(inv_std, inv_buf.shape)

    g_send[...] = jnp.zeros_like(g_send)
    for head in range(HEADS):
        g_send[head, :, :HEAD] = d_out[0, :, head * HEAD:(head + 1) * HEAD]
    g_sems = (g_ssem, g_rsem)

    def g_copy(step):
        to = lax.rem(me + step, SEQ)
        return remote(g_send.at[to], g_recv.at[me], g_sems, step, to)

    def g_arrival(step):
        origin = lax.rem(me - step + SEQ, SEQ)
        return remote(g_send.at[origin], g_recv.at[origin], g_sems, step, origin)

    def g_start(step, carry):
        g_copy(step).start()
        return carry

    for part in range(3):
        w_rows[part, :HEAD] = w[part * HEAD:(part + 1) * HEAD]
        w_rows[part, HEAD:] = jnp.zeros((SURE - HEAD, D), BF)
    w_side[:, :, :, SURE:, :] = jnp.zeros((2, SIDE, 3, LANES - SURE, D), BF)
    for axis in (0, 1):
        w_side[axis, place[axis], :, :SURE, :] = w_rows[...]
    w3[...] = w_side[0, y].reshape(WIDE, D).T
    g_recv[me] = g_send[me]

    lane = lax.broadcasted_iota(jnp.int32, (1, WIDE), 1)
    column_scale = jnp.where(lane < LANES, SCALE * LOG2E, 1.0).astype(F32)

    def project(offsets):
        places = [(half, tree.slot(half, *offset)) for half in (0, 1) for offset in offsets]
        rows = jnp.concatenate([blocks[at] for at in places], axis=0)
        out = (dot(rows, w3[...]) * column_scale).astype(BF)
        for at, (half, slot) in enumerate(places):
            qkv[half, slot] = out[at * HALF:(at + 1) * HALF]

    project([(0, 0)])
    tree.rest(project, lambda: lax.fori_loop(1, SEQ, g_start, 0))

    def arrival(ref, sems, axis, step):
        part = ref.at[axis, wrap(place[axis] - step, SIDE)]
        return remote(part, part, sems, (axis, step), peer(axis, step))

    def g_wait(step, carry):
        g_copy(step).wait_send()
        g_arrival(step).wait_recv()
        return carry

    lax.fori_loop(1, SEQ, g_wait, 0)
    for axis in (0, 1):
        for sign in (1, -1):
            w_own(axis, sign).start()
    hot = (lax.broadcasted_iota(jnp.int32, (PACKED, HEADS * TAIL), 0) == rank[...]).astype(BF)
    turned = [column * SIDE + row for row in range(SIDE) for column in range(SIDE)]
    g[:FIRST] = g_recv[:, :HALF, :].reshape(FIRST, LANES)
    for at, owner in enumerate(turned):
        g[FIRST + at * MORE:FIRST + (at + 1) * MORE] = g_recv[owner, HALF:SURE, :]
    g_tail = jnp.concatenate([g_recv[owner, SURE:, :] for owner in turned], axis=0)
    g[PACK_AT:] = dot(hot, g_tail).astype(BF)

    tail = dot(hot, qkv[1, :, MORE:, :].reshape(HEADS * TAIL, WIDE)).astype(BF)
    for part, ref in enumerate((q, k, v)):
        lanes = slice(part * LANES, (part + 1) * LANES)
        ref[:FIRST] = qkv[0, :, :, lanes].reshape(FIRST, LANES)
        ref[FIRST:PACK_AT] = qkv[1, :, :MORE, lanes].reshape(SEQ * MORE, LANES)
        ref[PACK_AT:] = tail[:, lanes]
    lane = lax.broadcasted_iota(jnp.int32, (LIVE, LANES), 1)
    ones = (lane == HEAD) | (lane == HEAD + 1)
    v[...] = jnp.where(ones, 1.0, v[...].astype(F32)).astype(BF)
    kt[...] = k[...].T
    vt[...] = v[...].T

    def between(at):
        @pl.when(at == 5)
        def _():
            for axis in (0, 1):
                for sign in (1, -1):
                    w_from(axis, sign).wait_recv()
                    w_onward(axis, sign).start()

    attend(q, kt, k, v, vt, g, att, dq, dkt, dvt, between)

    dk = (dkt[...].T * LN2).astype(BF)
    dv = dvt[...].T.astype(BF)
    packed = jnp.concatenate([dq[PACK_AT:], dk[PACK_AT:], dv[PACK_AT:], att[PACK_AT:]], axis=1)
    loose = dot(hot, packed, 0, 0).astype(BF).reshape(SIDE, SIDE, TAIL, 4 * LANES)
    for part, value in enumerate((dq, dk, dv)):
        lanes = slice(part * LANES, (part + 1) * LANES)
        d_send[0, :, :, :, lanes] = value[:FIRST].reshape(SIDE, SIDE, HALF, LANES)
        d_send[1, :, :, :MORE, lanes] = value[FIRST:PACK_AT].reshape(SIDE, SIDE, MORE, LANES)
    d_send[1, :, :, MORE:, :] = loose[..., :WIDE]

    d_sems = (d_ssem, d_rsem)

    def d_copy(axis, step):
        to = wrap(place[axis] + step, SIDE)
        return remote(
            d_send.at[axis, to], d_recv.at[axis, place[axis]], d_sems, (axis, step), peer(axis, step)
        )

    for step in (2, 1, 3):
        for axis in (0, 1):
            d_copy(axis, step).start()
    for axis in (0, 1):
        d_recv[axis, place[axis]] = d_send[axis, place[axis]]
    att_send[:, :HALF, :] = att[:FIRST].reshape(SEQ, HALF, LANES)
    for at, owner in enumerate(turned):
        att_send[owner, HALF:SURE, :] = att[FIRST + at * MORE:FIRST + (at + 1) * MORE]
        att_send[owner, SURE:, :] = loose[at // SIDE, at % SIDE, :, WIDE:]
    a_sems = (a_ssem, a_rsem)

    def a_copy(step):
        to = lax.rem(me + step, SEQ)
        return remote(att_send.at[to], att_recv.at[me], a_sems, step, to)

    def a_arrival(step):
        origin = lax.rem(me - step + SEQ, SEQ)
        return remote(att_send.at[origin], att_recv.at[origin], a_sems, step, origin)

    def a_start(step, carry):
        a_copy(step).start()
        return carry

    lax.fori_loop(1, SEQ, a_start, 0)
    att_recv[me] = att_send[me]

    for first, last in ((0, 512), (512, 1024), (1024, D)):
        dwt[:, first:last] = dot(
            d_send[...].reshape(SEQ * CAP, WIDE),
            blocks[:, :, :, first:last].reshape(SEQ * CAP, last - first), 0, 0,
        )

    def lanes_of(which):
        return pl.ds(pl.multiple_of(which * (D - HALF_LANES), LANES), HALF_LANES)

    pair_send[...] = dwt[:, lanes_of(1 - core)].astype(BF)
    c_sems = (c_ssem, c_rsem)
    pair_copy = remote(pair_send, pair_recv, c_sems, 0, other, "batch")
    pair_copy.start()

    z_sems = (z_ssem, z_rsem)

    def z_copy(phase, step):
        src = z_send.at[wrap(z + step, DEPTH)] if phase == 0 else z_all.at[z]
        dst = (z_recv if phase == 0 else z_all).at[z]
        return remote(src, dst, z_sems, (phase, step), above(step), "batch")

    def z_arrival(phase, step):
        ref = (z_recv if phase == 0 else z_all).at[wrap(z - step, DEPTH)]
        return remote(ref, ref, z_sems, (phase, step), above(step), "batch")

    p_sems = (p_ssem, p_rsem)

    def p_copy(axis, step):
        to = wrap(place[axis] + step, SIDE)
        return remote(
            part_send.at[axis, to], part_recv.at[axis, place[axis]], p_sems, (axis, step), peer(axis, step)
        )

    for axis in (0, 1):
        for sign in (1, -1):
            w_onward(axis, sign, True).wait_recv()
        for step in (1, 2, 3):
            arrival(d_recv, d_sems, axis, step).wait_recv()
        left = jnp.concatenate(
            [d_recv[axis, head].reshape(SIDE * HALF, WIDE) for head in range(SIDE)], axis=1
        )
        partial = dot(left, w_side[axis].reshape(SIDE * WIDE, D))
        part_send[1 - axis] = partial.astype(BF).reshape(SIDE, HALF, D)
        for step in (2, 1, 3):
            p_copy(1 - axis, step).start()
        if axis == 0:
            pair_copy.wait()
            z_send[...] = (dwt[:, lanes_of(core)] + pair_recv[...].astype(F32)).astype(BF).reshape(
                DEPTH, SHARD, HALF_LANES
            )
            for step in (4, 3, 5, 2, 6, 1, 7):
                z_copy(0, step).start()
            z_recv[z] = z_send[z]
    for axis in (0, 1):
        part_recv[axis, place[axis]] = part_send[axis, place[axis]]

    def a_wait(step, carry):
        a_copy(step).wait_send()
        a_arrival(step).wait_recv()
        return carry

    lax.fori_loop(1, SEQ, a_wait, 0)
    for head in range(HEADS):
        attn_out[0, :, head * HEAD:(head + 1) * HEAD] = att_recv[head, :, :HEAD]

    for step in range(1, DEPTH):
        z_arrival(0, step).wait_recv()
    total = z_recv[0].astype(F32)
    for at in range(1, DEPTH):
        total = total + z_recv[at].astype(F32)
    z_all[z] = total.astype(BF)
    for step in (4, 3, 5, 2, 6, 1, 7):
        z_copy(1, step).start()

    def o_copy(step):
        slot = wrap(z - step, DEPTH)
        return remote(z_all.at[slot], z_other.at[slot], (o_ssem, o_rsem), step, other, "batch")

    o_copy(0).start()

    for axis in (0, 1):
        for step in (1, 2, 3):
            arrival(part_recv, p_sems, axis, step).wait_recv()
    halves = []
    for axis in (1, 0):
        value = part_recv[axis, 0].astype(F32)
        for at in range(1, SIDE):
            value = value + part_recv[axis, at].astype(F32)
        halves.append(value)
    d_normed = jnp.concatenate(halves, axis=0)
    normed = normed_buf[...]
    d_picked = inv_buf[:, :1] * (
        d_normed
        - jnp.mean(d_normed, axis=1, keepdims=True)
        - normed * jnp.mean(d_normed * normed, axis=1, keepdims=True)
    )
    spread = (lax.broadcasted_iota(jnp.int32, (rows_buf.shape[0], CAP), 0) == index[...]).astype(BF)
    rows_buf[...] = dot(spread, d_picked.astype(BF)).astype(BF)
    store = pltpu.make_async_copy(rows_buf, d_tokens_out.at[0], out_sem)
    store.start()

    for step in (1, 7, 2, 6, 3, 5, 4):
        z_arrival(1, step).wait_recv()
        o_copy(step).start()
    for step in range(DEPTH):
        o_copy(step).wait()
    mine, theirs = (
        ref[...].astype(F32).reshape(WIDE, HALF_LANES) for ref in (z_all, z_other)
    )
    low = jnp.where(core == 0, mine, theirs)
    high = jnp.where(core == 0, theirs, mine)
    overlap = 2 * HALF_LANES - D
    for part in range(3):
        rows = slice(part * HEAD, (part + 1) * HEAD)
        padded = slice(part * LANES, part * LANES + HEAD)
        d_wqkv[rows, :HALF_LANES] = low[padded]
        d_wqkv[rows, HALF_LANES:] = high[padded, overlap:]

    for axis in (0, 1):
        for sign in (1, -1):
            w_own(axis, sign).wait_send()
            w_onward(axis, sign).wait_send()
        for step in (1, 2, 3):
            d_copy(axis, step).wait_send()
            p_copy(axis, step).wait_send()
    for step in range(1, DEPTH):
        z_copy(0, step).wait_send()
        z_copy(1, step).wait_send()
    tree.finish()
    store.wait()


def layer_call(tokens, w, d_out, rank, index):
    vmem = pl.BlockSpec(memory_space=VMEM)
    anywhere = pl.BlockSpec(memory_space=pl.ANY)
    dma = pltpu.SemaphoreType.DMA
    positions = tokens.shape[1]
    pair = [dma((2, SIDE)), dma((2, SIDE))]
    return pl.pallas_call(
        layer_kernel,
        out_shape=(
            jax.ShapeDtypeStruct((1, CAP, D), BF),
            jax.ShapeDtypeStruct((1, positions, D), BF),
            jax.ShapeDtypeStruct((3 * HEAD, D), F32),
        ),
        in_specs=[anywhere] + [vmem] * 4,
        out_specs=(vmem, anywhere, vmem),
        scratch_shapes=[
            VMEM((positions, D), BF),
            VMEM((2, SEQ, HALF, D), BF),
            VMEM((CAP, D), F32),
            VMEM((CAP, LANES), F32),
            VMEM((3, SURE, D), BF),
            VMEM((2, SIDE, 3, LANES, D), BF),
            VMEM((D, WIDE), BF),
            VMEM((SEQ, CAP, LANES), BF),
            VMEM((SEQ, CAP, LANES), BF),
            VMEM((2, SEQ, HALF, WIDE), BF),
            VMEM((LIVE, LANES), BF),
            VMEM((LIVE, LANES), BF),
            VMEM((LIVE, LANES), BF),
            VMEM((LIVE, LANES), BF),
            VMEM((LANES, LIVE), BF),
            VMEM((LANES, LIVE), BF),
            VMEM((LIVE, LANES), BF),
            VMEM((LIVE, LANES), BF),
            VMEM((LANES, LIVE), F32),
            VMEM((LANES, LIVE), F32),
            VMEM((2, SIDE, SIDE, HALF, WIDE), BF),
            VMEM((SEQ, CAP, LANES), BF),
            VMEM((SEQ, CAP, LANES), BF),
            VMEM((2, SIDE, SIDE, HALF, WIDE), BF),
            VMEM((2, SIDE, HALF, D), BF),
            VMEM((2, SIDE, HALF, D), BF),
            VMEM((WIDE, D), F32),
            VMEM((WIDE, HALF_LANES), BF),
            VMEM((WIDE, HALF_LANES), BF),
            VMEM((DEPTH, SHARD, HALF_LANES), BF),
            VMEM((DEPTH, SHARD, HALF_LANES), BF),
            VMEM((DEPTH, SHARD, HALF_LANES), BF),
            VMEM((DEPTH, SHARD, HALF_LANES), BF),
            dma((2, len(KEYS))), dma((2, len(KEYS))),
            dma((SEQ,)), dma((SEQ,)),
            *pair, *pair, *pair,
            dma((SEQ,)), dma((SEQ,)),
            dma((2,)), dma((2,)),
            dma((2, DEPTH)), dma((2, DEPTH)),
            dma((DEPTH,)), dma((DEPTH,)),
            dma, dma,
        ],
        compiler_params=pltpu.CompilerParams(
            collective_id=1, has_side_effects=True, vmem_limit_bytes=VMEM_BYTES
        ),
        name="layer",
    )(tokens, w, d_out, rank, index)


def per_device(tokens, w_qkv, vis_index, counts, d_out):
    extra = (counts[0] - SURE).reshape(SIDE, SIDE).T.reshape(SEQ)
    order = jnp.arange(SEQ, dtype=jnp.int32)
    before = jnp.sum(jnp.where(order[None, :] < order[:, None], extra[None, :], 0), axis=1)
    within = jnp.arange(TAIL, dtype=jnp.int32)
    rank = jnp.where(within[None, :] < extra[:, None], before[:, None] + within[None, :], -1)
    rank = rank.reshape(1, SEQ * TAIL).astype(jnp.int32)
    attn_out, d_tokens, d_wqkv = layer_call(tokens, w_qkv.T, d_out, rank, vis_index)
    return attn_out, d_tokens, d_wqkv.T


def solution(mesh):
    placed = (
        P("batch", "seq", None),
        P(None, "seq"),
        P("batch", "seq"),
        P("batch", None),
        P("batch", "seq", None),
    )
    return jax.shard_map(
        per_device,
        mesh=mesh,
        in_specs=placed,
        out_specs=(P("batch", "seq", None), P("batch", "seq", None), P(None, "seq")),
        check_vma=False,
    )
```

time: 163 us -> 144 us (0.88)
  Pallas kernels: 153 us -> 135 us
    pallas_call x2 -> x1, Pallas kernels: 153 us -> 135 us  [layer_call(): pl.pallas_call(layer_kernel, out_shape=(jax.ShapeDtypeStruct((1, CAP, D),...]
    pallas_call x1 -> x0, local copies, waits for them, and re-layouts: 2.95 us -> none  [attend_call(): pl.pallas_call(attend_kernel, out_shape=(jax.ShapeDtypeStruct((1, CAP, D)...]
    unnamed x7 -> x5, local copies, waits for them, and re-layouts: 4.62 us -> 6.65 us
where the time goes in v2:
time: 144 us
  Pallas kernels  135 us (94%)
  local copies, waits for them, and re-layouts  7.6 us (5%)
    pallas_call x1, Pallas kernels, layer_call(): pl.pallas_call(layer_kernel, out_shape=(jax.ShapeDtypeStruct((1, CAP, D),...  135 us
    unnamed x5, local copies, waits for them, and re-layouts  6.65 us

profile of v2, /device:TPU:1, one launch (start us, length us, event | category | flops | bytes accessed | tf_op | source)
XLA Modules:
  0.0 143.9 jit_solution(10758192874746940662)
XLA Ops:
  0.6 0.7 add_reduce_fusion
  1.3 0.1 sub.6
  1.4 0.1 copy.9
  1.5 0.1 lt.39
  1.6 0.1 select_reduce_fusion
  1.7 0.1 add_select_fusion
  1.8 0.7 select_n.20.rank
  2.4 134.8 %layer.1 = (bf16[1,160,1408]{2,1,0:T(8,128)(2,1)}, bf16[1,1024,1408]{2,1,0:T(8,128)(2,1)}, f32[264,1408]{1,0:T(8,128)}) custom-call(bf16[1,1024,1408]{2,1,0:T(8,128)(2,1)} %tokens_in.1, bf16[264,1408]{1,0:T(8,128)(2,1)} %bitcast.4, bf16[1,160,1408]{2,1,0:T(8,128)(2,1)} %d_out.1, s32[1,1024]{1,0:T(1,128)} %select_n.20.rank, s32[1,160]{1,0:T(1,128)} %index.1), custom_call_target="tpu_custom_call" | custom-call | tf_op jit(solution)/shard_map/layer/pallas_call | solution.py:540
  137.2 1.8 %copy.13 = bf16[1,160,1408]{2,1,0:T(8,128)(2,1)} copy(bf16[1,160,1408]{2,1,0:T(8,128)(2,1)} %get-tuple-element.12) | data formatting | bytes 901120
  139.0 0.0 copy-start
  139.0 3.7 %copy.14 = bf16[1,1024,1408]{2,1,0:T(8,128)(2,1)} copy(bf16[1,1024,1408]{2,1,0:T(8,128)(2,1)} %get-tuple-element.13) | data formatting | bytes 5767168
  142.7 0.0 copy-done
  142.8 1.1 copy.15
Async XLA Ops:
  139.0 3.7 %copy-start = (f32[264,1408]{1,0:T(8,128)S(1)}, f32[264,1408]{1,0:T(8,128)}, u32[]{:S(2)}) copy-start(f32[264,1408]{1,0:T(8,128)} %get-tuple-element.8) | copy-start | bytes 4460548

commit v3 on v2

--- a/solution.py
+++ b/solution.py
@@ -28,6 +28,8 @@
 F32 = jnp.float32
 VMEM = pltpu.VMEM
 VMEM_BYTES = 62 * 2**20
+CHUNKS = 4
+CHUNK = 1024 // CHUNKS
 
 
 def dot(left, right, left_dim=1, right_dim=0):
@@ -116,7 +118,7 @@
         for s in (1, -1):
             self.start("P2", "o", s)
 
-    def rest(self, done, late):
+    def rest(self, done):
         for s in (1, -1):
             self.arrive("P1", s)
             self.start("P1f", s)
@@ -142,7 +144,6 @@
                 self.arrive("P2", j, s)
                 if ("P2f", j, s) in IDS:
                     self.start("P2f", j, s)
-        late()
         for s in (1, -1):
             self.arrive("P2f", "o", s)
         done([(2, -1), (2, 1), (0, 2)])
@@ -201,10 +202,10 @@
 def layer_kernel(
     tokens_in, w, d_out, rank, index,
     attn_out, d_tokens_out, d_wqkv,
-    rows_buf, blocks, normed_buf, inv_buf, w_rows, w_side, w3, g_send, g_recv, qkv,
+    rows_buf, blocks, normed_buf, inv_buf, w_side, w3, g_send, g_recv, qkv,
     q, k, v, g, kt, vt, att, dq, dkt, dvt,
     d_send, att_send, att_recv, d_recv, part_send, part_recv,
-    dwt, pair_send, pair_recv, z_send, z_recv, z_all, z_other,
+    turned_d, own_sum, pair_send, pair_recv, z_send, z_recv, z_all, z_other,
     t_ssem, t_rsem, g_ssem, g_rsem, w_ssem, w_rsem,
     d_ssem, d_rsem, p_ssem, p_rsem, a_ssem, a_rsem, c_ssem, c_rsem, z_ssem, z_rsem, o_ssem, o_rsem,
     in_sem, out_sem,
@@ -225,8 +226,12 @@
 
     other = batch + 1 - 2 * core
 
-    fetch = pltpu.make_async_copy(tokens_in.at[0], rows_buf, in_sem)
-    fetch.start()
+    def fetch(part):
+        rows = pl.ds(part * CHUNK, CHUNK)
+        return pltpu.make_async_copy(tokens_in.at[0, rows], rows_buf.at[rows], in_sem.at[part])
+
+    for part in range(CHUNKS):
+        fetch(part).start()
     barrier = pltpu.get_barrier_semaphore()
     for step in range(1, SEQ):
         pl.semaphore_signal(
@@ -244,28 +249,43 @@
             device_id={where: to}, device_id_type=MESH,
         )
 
-    w_sems = (w_ssem, w_rsem)
-
-    def w_own(axis, sign):
-        dst = w_side.at[axis, place[axis], :, pl.ds(0, SURE)]
-        return remote(w_rows, dst, w_sems, (axis, (1 - sign) // 2), peer(axis, sign))
-
-    def w_from(axis, sign):
-        dst = w_side.at[axis, wrap(place[axis] - sign, SIDE), :, pl.ds(0, SURE)]
-        return remote(w_rows, dst, w_sems, (axis, (1 - sign) // 2), peer(axis, -sign))
-
-    def w_onward(axis, sign, receiver=False):
-        origin = wrap(place[axis] - (2 * sign if receiver else sign), SIDE)
-        ref = w_side.at[axis, origin, :, pl.ds(0 if sign == 1 else SURE // 2, SURE // 2)]
-        return remote(ref, ref, w_sems, (axis, 2 + (1 - sign) // 2), peer(axis, sign))
-
-    fetch.wait()
-    spread = (lax.broadcasted_iota(jnp.int32, (rows_buf.shape[0], CAP), 0) == index[...]).astype(BF)
-    picked = dot(spread, rows_buf[...], 0, 0)
+    g_send[...] = jnp.zeros_like(g_send)
+    for head in range(HEADS):
+        g_send[head, :, :HEAD] = d_out[0, :, head * HEAD:(head + 1) * HEAD]
+    g_sems = (g_ssem, g_rsem)
+
+    def g_copy(step):
+        to = lax.rem(me + step, SEQ)
+        return remote(g_send.at[to], g_recv.at[me], g_sems, step, to)
+
+    def g_arrival(step):
+        origin = lax.rem(me - step + SEQ, SEQ)
+        return remote(g_send.at[origin], g_recv.at[origin], g_sems, step, origin)
+
+    def g_start(step, carry):
+        g_copy(step).start()
+        return carry
+
+    pl.semaphore_wait(barrier, SEQ - 1 + DEPTH)
+    lax.fori_loop(1, SEQ, g_start, 0)
+
+    column = jnp.broadcast_to(index[...], (LANES, CAP)).T
+    lane = lax.broadcasted_iota(jnp.int32, (CAP, LANES), 1)
+    picked = None
+    for part in range(CHUNKS):
+        hot = jnp.concatenate(
+            [
+                (column == lane + (part * CHUNK + first)).astype(BF)
+                for first in range(0, CHUNK, LANES)
+            ],
+            axis=1,
+        )
+        fetch(part).wait()
+        rows = dot(hot, rows_buf[part * CHUNK:(part + 1) * CHUNK])
+        picked = rows if picked is None else picked + rows
     centred = picked - jnp.mean(picked, axis=1, keepdims=True)
     inv_std = lax.rsqrt(jnp.mean(centred * centred, axis=1, keepdims=True) + EPSILON)
     normed = centred * inv_std
-    pl.semaphore_wait(barrier, SEQ - 1 + DEPTH)
     blocks[0, me] = normed[:HALF].astype(BF)
     blocks[1, x * SIDE + y] = normed[HALF:].astype(BF)
     tree = Tree(me, 1 - 2 * core, blocks, t_ssem, t_rsem)
@@ -273,29 +293,11 @@
     normed_buf[...] = normed
     inv_buf[...] = jnp.broadcast_to(inv_std, inv_buf.shape)
 
-    g_send[...] = jnp.zeros_like(g_send)
-    for head in range(HEADS):
-        g_send[head, :, :HEAD] = d_out[0, :, head * HEAD:(head + 1) * HEAD]
-    g_sems = (g_ssem, g_rsem)
-
-    def g_copy(step):
-        to = lax.rem(me + step, SEQ)
-        return remote(g_send.at[to], g_recv.at[me], g_sems, step, to)
-
-    def g_arrival(step):
-        origin = lax.rem(me - step + SEQ, SEQ)
-        return remote(g_send.at[origin], g_recv.at[origin], g_sems, step, origin)
-
-    def g_start(step, carry):
-        g_copy(step).start()
-        return carry
-
-    for part in range(3):
-        w_rows[part, :HEAD] = w[part * HEAD:(part + 1) * HEAD]
-        w_rows[part, HEAD:] = jnp.zeros((SURE - HEAD, D), BF)
     w_side[:, :, :, SURE:, :] = jnp.zeros((2, SIDE, 3, LANES - SURE, D), BF)
     for axis in (0, 1):
-        w_side[axis, place[axis], :, :SURE, :] = w_rows[...]
+        for part in range(3):
+            w_side[axis, place[axis], part, :HEAD] = w[part * HEAD:(part + 1) * HEAD]
+            w_side[axis, place[axis], part, HEAD:SURE] = jnp.zeros((SURE - HEAD, D), BF)
     w3[...] = w_side[0, y].reshape(WIDE, D).T
     g_recv[me] = g_send[me]
 
@@ -310,7 +312,34 @@
             qkv[half, slot] = out[at * HALF:(at + 1) * HALF]
 
     project([(0, 0)])
-    tree.rest(project, lambda: lax.fori_loop(1, SEQ, g_start, 0))
+    tree.rest(project)
+
+    w_sems = (w_ssem, w_rsem)
+    way = 1 - 2 * core
+    share = SURE // 2
+    PIECE = {0: (0, share), 1: (0, 32), -1: (32, share - 32)}
+
+    def w_part(axis, step, piece, whose):
+        start, rows = PIECE[piece]
+        start = pl.multiple_of(whose * share + start, 16)
+        return w_side.at[axis, wrap(place[axis] + step, SIDE), :, pl.ds(start, rows)]
+
+    def w_move(ref, axis, slot, sign, to, where="seq"):
+        return remote(ref, ref, w_sems, (axis, slot + (1 - sign) // 2), to, where)
+
+    def w_own(axis, sign):
+        return w_move(w_part(axis, 0, 0, core), axis, 0, sign, peer(axis, sign * way))
+
+    def w_from(axis, sign):
+        return w_move(w_part(axis, -sign * way, 0, core), axis, 0, sign, peer(axis, -sign * way))
+
+    def w_onward(axis, sign, hops=1):
+        return w_move(w_part(axis, -hops * sign * way, sign, core), axis, 2, sign, peer(axis, sign * way))
+
+    def w_across(axis, sign, far, receiver=False):
+        whose, side = (1 - core, -way) if receiver else (core, way)
+        step, piece = (-2 * sign * side, sign) if far else (-sign * side, 0)
+        return w_move(w_part(axis, step, piece, whose), axis, 6 if far else 4, sign, other, "batch")
 
     def arrival(ref, sems, axis, step):
         part = ref.at[axis, wrap(place[axis] - step, SIDE)]
@@ -345,13 +374,49 @@
     kt[...] = k[...].T
     vt[...] = v[...].T
 
+    a_sems = (a_ssem, a_rsem)
+
+    def a_part(ref, half, node):
+        return ref.at[node, pl.ds(half * HALF, HALF)]
+
+    def a_copy(half, step):
+        to = lax.rem(me + step, SEQ)
+        return remote(a_part(att_send, half, to), a_part(att_recv, half, me), a_sems, (half, step), to)
+
+    def a_arrival(half, step):
+        origin = lax.rem(me - step + SEQ, SEQ)
+        part = a_part(att_recv, half, origin)
+        return remote(part, part, a_sems, (half, step), origin)
+
+    def a_start(half):
+        def one(step, carry):
+            a_copy(half, step).start()
+            return carry
+
+        lax.fori_loop(1, SEQ, one, 0)
+
     def between(at):
-        @pl.when(at == 5)
+        @pl.when(at == 4)
         def _():
             for axis in (0, 1):
                 for sign in (1, -1):
                     w_from(axis, sign).wait_recv()
                     w_onward(axis, sign).start()
+            for axis in (0, 1):
+                for sign in (1, -1):
+                    w_across(axis, sign, False).start()
+
+        @pl.when(at == FIRST // QB)
+        def _():
+            att_send[:, :HALF, :] = att[:FIRST].reshape(SEQ, HALF, LANES)
+            a_start(0)
+
+        @pl.when(at == LIVE // QB - 1)
+        def _():
+            for axis in (0, 1):
+                for sign in (1, -1):
+                    w_onward(axis, sign, 2).wait_recv()
+                    w_across(axis, sign, True).start()
 
     attend(q, kt, k, v, vt, g, att, dq, dkt, dvt, between)
 
@@ -378,40 +443,25 @@
             d_copy(axis, step).start()
     for axis in (0, 1):
         d_recv[axis, place[axis]] = d_send[axis, place[axis]]
-    att_send[:, :HALF, :] = att[:FIRST].reshape(SEQ, HALF, LANES)
+
+    def lanes_of(which):
+        return pl.ds(pl.multiple_of(which * (D - HALF_LANES), LANES), HALF_LANES)
+
+    turned_d[...] = d_send[...].reshape(SEQ * CAP, WIDE).T
+
+    def product(which):
+        return dot(turned_d[...], blocks[:, :, :, lanes_of(which)].reshape(SEQ * CAP, HALF_LANES))
+
+    pair_send[...] = product(1 - core).astype(BF)
+    c_sems = (c_ssem, c_rsem)
+    pair_copy = remote(pair_send, pair_recv, c_sems, 0, other, "batch")
+    pair_copy.start()
     for at, owner in enumerate(turned):
         att_send[owner, HALF:SURE, :] = att[FIRST + at * MORE:FIRST + (at + 1) * MORE]
         att_send[owner, SURE:, :] = loose[at // SIDE, at % SIDE, :, WIDE:]
-    a_sems = (a_ssem, a_rsem)
-
-    def a_copy(step):
-        to = lax.rem(me + step, SEQ)
-        return remote(att_send.at[to], att_recv.at[me], a_sems, step, to)
-
-    def a_arrival(step):
-        origin = lax.rem(me - step + SEQ, SEQ)
-        return remote(att_send.at[origin], att_recv.at[origin], a_sems, step, origin)
-
-    def a_start(step, carry):
-        a_copy(step).start()
-        return carry
-
-    lax.fori_loop(1, SEQ, a_start, 0)
+    a_start(1)
     att_recv[me] = att_send[me]
-
-    for first, last in ((0, 512), (512, 1024), (1024, D)):
-        dwt[:, first:last] = dot(
-            d_send[...].reshape(SEQ * CAP, WIDE),
-            blocks[:, :, :, first:last].reshape(SEQ * CAP, last - first), 0, 0,
-        )
-
-    def lanes_of(which):
-        return pl.ds(pl.multiple_of(which * (D - HALF_LANES), LANES), HALF_LANES)
-
-    pair_send[...] = dwt[:, lanes_of(1 - core)].astype(BF)
-    c_sems = (c_ssem, c_rsem)
-    pair_copy = remote(pair_send, pair_recv, c_sems, 0, other, "batch")
-    pair_copy.start()
+    own_sum[...] = product(core)
 
     z_sems = (z_ssem, z_rsem)
 
@@ -424,6 +474,14 @@
         ref = (z_recv if phase == 0 else z_all).at[wrap(z - step, DEPTH)]
         return remote(ref, ref, z_sems, (phase, step), above(step), "batch")
 
+    pair_copy.wait()
+    z_send[...] = (own_sum[...] + pair_recv[...].astype(F32)).astype(BF).reshape(
+        DEPTH, SHARD, HALF_LANES
+    )
+    for step in (4, 3, 5, 2, 6, 1, 7):
+        z_copy(0, step).start()
+    z_recv[z] = z_send[z]
+
     p_sems = (p_ssem, p_rsem)
 
     def p_copy(axis, step):
@@ -434,7 +492,8 @@
 
     for axis in (0, 1):
         for sign in (1, -1):
-            w_onward(axis, sign, True).wait_recv()
+            w_across(axis, sign, False, True).wait_recv()
+            w_across(axis, sign, True, True).wait_recv()
         for step in (1, 2, 3):
             arrival(d_recv, d_sems, axis, step).wait_recv()
         left = jnp.concatenate(
@@ -444,20 +503,13 @@
         part_send[1 - axis] = partial.astype(BF).reshape(SIDE, HALF, D)
         for step in (2, 1, 3):
             p_copy(1 - axis, step).start()
-        if axis == 0:
-            pair_copy.wait()
-            z_send[...] = (dwt[:, lanes_of(core)] + pair_recv[...].astype(F32)).astype(BF).reshape(
-                DEPTH, SHARD, HALF_LANES
-            )
-            for step in (4, 3, 5, 2, 6, 1, 7):
-                z_copy(0, step).start()
-            z_recv[z] = z_send[z]
     for axis in (0, 1):
         part_recv[axis, place[axis]] = part_send[axis, place[axis]]
 
     def a_wait(step, carry):
-        a_copy(step).wait_send()
-        a_arrival(step).wait_recv()
+        for half in (0, 1):
+            a_copy(half, step).wait_send()
+            a_arrival(half, step).wait_recv()
         return carry
 
     lax.fori_loop(1, SEQ, a_wait, 0)
@@ -521,6 +573,8 @@
         for sign in (1, -1):
             w_own(axis, sign).wait_send()
             w_onward(axis, sign).wait_send()
+            w_across(axis, sign, False).wait_send()
+            w_across(axis, sign, True).wait_send()
         for step in (1, 2, 3):
             d_copy(axis, step).wait_send()
             p_copy(axis, step).wait_send()
@@ -551,7 +605,6 @@
             VMEM((2, SEQ, HALF, D), BF),
             VMEM((CAP, D), F32),
             VMEM((CAP, LANES), F32),
-            VMEM((3, SURE, D), BF),
             VMEM((2, SIDE, 3, LANES, D), BF),
             VMEM((D, WIDE), BF),
             VMEM((SEQ, CAP, LANES), BF),
@@ -573,7 +626,8 @@
             VMEM((2, SIDE, SIDE, HALF, WIDE), BF),
             VMEM((2, SIDE, HALF, D), BF),
             VMEM((2, SIDE, HALF, D), BF),
-            VMEM((WIDE, D), F32),
+            VMEM((WIDE, SEQ * CAP), BF),
+            VMEM((WIDE, HALF_LANES), F32),
             VMEM((WIDE, HALF_LANES), BF),
             VMEM((WIDE, HALF_LANES), BF),
             VMEM((DEPTH, SHARD, HALF_LANES), BF),
@@ -582,12 +636,13 @@
             VMEM((DEPTH, SHARD, HALF_LANES), BF),
             dma((2, len(KEYS))), dma((2, len(KEYS))),
             dma((SEQ,)), dma((SEQ,)),
-            *pair, *pair, *pair,
-            dma((SEQ,)), dma((SEQ,)),
+            dma((2, 8)), dma((2, 8)),
+            *pair, *pair,
+            dma((2, SEQ)), dma((2, SEQ)),
             dma((2,)), dma((2,)),
             dma((2, DEPTH)), dma((2, DEPTH)),
             dma((DEPTH,)), dma((DEPTH,)),
-            dma, dma,
+            dma((CHUNKS,)), dma,
         ],
         compiler_params=pltpu.CompilerParams(
             collective_id=1, has_side_effects=True, vmem_limit_bytes=VMEM_BYTES

time: 144 us -> 129 us (0.90)
  Pallas kernels: 135 us -> 120 us
    pallas_call x1, Pallas kernels: 135 us -> 120 us  [layer_call(): pl.pallas_call(layer_kernel, out_shape=(jax.ShapeDtypeStruct((1, CAP, D),...]
where the time goes in v3:
time: 129 us
  Pallas kernels  120 us (93%)
  local copies, waits for them, and re-layouts  7.6 us (6%)
    pallas_call x1, Pallas kernels, layer_call(): pl.pallas_call(layer_kernel, out_shape=(jax.ShapeDtypeStruct((1, CAP, D),...  120 us
    unnamed x5, local copies, waits for them, and re-layouts  6.65 us

profile of v3, /device:TPU:1, one launch (start us, length us, event | category | flops | bytes accessed | tf_op | source)
XLA Modules:
  0.0 129.1 jit_solution(16802691117787617444)
XLA Ops:
  0.6 0.7 add_reduce_fusion
  1.3 0.1 sub.6
  1.4 0.1 copy.9
  1.5 0.1 lt.39
  1.6 0.1 select_reduce_fusion
  1.7 0.1 add_select_fusion
  1.8 0.7 select_n.20.rank
  2.4 120.0 %layer.1 = (bf16[1,160,1408]{2,1,0:T(8,128)(2,1)}, bf16[1,1024,1408]{2,1,0:T(8,128)(2,1)}, f32[264,1408]{1,0:T(8,128)}) custom-call(bf16[1,1024,1408]{2,1,0:T(8,128)(2,1)} %tokens_in.1, bf16[264,1408]{1,0:T(8,128)(2,1)} %bitcast.4, bf16[1,160,1408]{2,1,0:T(8,128)(2,1)} %d_out.1, s32[1,1024]{1,0:T(1,128)} %select_n.20.rank, s32[1,160]{1,0:T(1,128)} %index.1), custom_call_target="tpu_custom_call" | custom-call | tf_op jit(solution)/shard_map/layer/pallas_call | solution.py:594
  122.5 1.8 %copy.13 = bf16[1,160,1408]{2,1,0:T(8,128)(2,1)} copy(bf16[1,160,1408]{2,1,0:T(8,128)(2,1)} %get-tuple-element.12) | data formatting | bytes 901120
  124.3 0.0 copy-start
  124.3 3.7 %copy.14 = bf16[1,1024,1408]{2,1,0:T(8,128)(2,1)} copy(bf16[1,1024,1408]{2,1,0:T(8,128)(2,1)} %get-tuple-element.13) | data formatting | bytes 5767168
  128.0 0.0 copy-done
  128.0 1.1 copy.15
Async XLA Ops:
  124.3 3.7 %copy-start = (f32[264,1408]{1,0:T(8,128)S(1)}, f32[264,1408]{1,0:T(8,128)}, u32[]{:S(2)}) copy-start(f32[264,1408]{1,0:T(8,128)} %get-tuple-element.8) | copy-start | bytes 4460548

commit v4 on v3

--- a/solution.py
+++ b/solution.py
@@ -200,15 +200,15 @@
 
 
 def layer_kernel(
-    tokens_in, w, d_out, rank, index,
-    attn_out, d_tokens_out, d_wqkv,
+    tokens_in, w, d_out, counts, index,
+    attn_out, d_rows, d_wqkv,
     rows_buf, blocks, normed_buf, inv_buf, w_side, w3, g_send, g_recv, qkv,
     q, k, v, g, kt, vt, att, dq, dkt, dvt,
     d_send, att_send, att_recv, d_recv, part_send, part_recv,
     turned_d, own_sum, pair_send, pair_recv, z_send, z_recv, z_all, z_other,
     t_ssem, t_rsem, g_ssem, g_rsem, w_ssem, w_rsem,
     d_ssem, d_rsem, p_ssem, p_rsem, a_ssem, a_rsem, c_ssem, c_rsem, z_ssem, z_rsem, o_ssem, o_rsem,
-    in_sem, out_sem,
+    in_sem,
 ):
     me = lax.axis_index("seq")
     batch = lax.axis_index("batch")
@@ -354,8 +354,16 @@
     for axis in (0, 1):
         for sign in (1, -1):
             w_own(axis, sign).start()
-    hot = (lax.broadcasted_iota(jnp.int32, (PACKED, HEADS * TAIL), 0) == rank[...]).astype(BF)
     turned = [column * SIDE + row for row in range(SIDE) for column in range(SIDE)]
+    slot = lax.broadcasted_iota(jnp.int32, (1, HEADS * TAIL), 1)
+    rank = jnp.full_like(slot, -1)
+    before = 0
+    for at, owner in enumerate(turned):
+        extra = counts[0, owner] - SURE
+        within = slot - at * TAIL
+        rank = jnp.where((within >= 0) & (within < extra), before + within, rank)
+        before = before + extra
+    hot = (lax.broadcasted_iota(jnp.int32, (PACKED, HEADS * TAIL), 0) == rank).astype(BF)
     g[:FIRST] = g_recv[:, :HALF, :].reshape(FIRST, LANES)
     for at, owner in enumerate(turned):
         g[FIRST + at * MORE:FIRST + (at + 1) * MORE] = g_recv[owner, HALF:SURE, :]
@@ -547,10 +555,7 @@
         - jnp.mean(d_normed, axis=1, keepdims=True)
         - normed * jnp.mean(d_normed * normed, axis=1, keepdims=True)
     )
-    spread = (lax.broadcasted_iota(jnp.int32, (rows_buf.shape[0], CAP), 0) == index[...]).astype(BF)
-    rows_buf[...] = dot(spread, d_picked.astype(BF)).astype(BF)
-    store = pltpu.make_async_copy(rows_buf, d_tokens_out.at[0], out_sem)
-    store.start()
+    d_rows[...] = d_picked.astype(BF)
 
     for step in (1, 7, 2, 6, 3, 5, 4):
         z_arrival(1, step).wait_recv()
@@ -558,7 +563,7 @@
     for step in range(DEPTH):
         o_copy(step).wait()
     mine, theirs = (
-        ref[...].astype(F32).reshape(WIDE, HALF_LANES) for ref in (z_all, z_other)
+        ref[...].reshape(WIDE, HALF_LANES) for ref in (z_all, z_other)
     )
     low = jnp.where(core == 0, mine, theirs)
     high = jnp.where(core == 0, theirs, mine)
@@ -582,10 +587,9 @@
         z_copy(0, step).wait_send()
         z_copy(1, step).wait_send()
     tree.finish()
-    store.wait()
-
-
-def layer_call(tokens, w, d_out, rank, index):
+
+
+def layer_call(tokens, w, d_out, counts, index):
     vmem = pl.BlockSpec(memory_space=VMEM)
     anywhere = pl.BlockSpec(memory_space=pl.ANY)
     dma = pltpu.SemaphoreType.DMA
@@ -595,11 +599,11 @@
         layer_kernel,
         out_shape=(
             jax.ShapeDtypeStruct((1, CAP, D), BF),
-            jax.ShapeDtypeStruct((1, positions, D), BF),
-            jax.ShapeDtypeStruct((3 * HEAD, D), F32),
+            jax.ShapeDtypeStruct((CAP, D), BF),
+            jax.ShapeDtypeStruct((3 * HEAD, D), BF),
         ),
-        in_specs=[anywhere] + [vmem] * 4,
-        out_specs=(vmem, anywhere, vmem),
+        in_specs=[anywhere, vmem, vmem, pl.BlockSpec(memory_space=pltpu.SMEM), vmem],
+        out_specs=(vmem,) * 3,
         scratch_shapes=[
             VMEM((positions, D), BF),
             VMEM((2, SEQ, HALF, D), BF),
@@ -642,23 +646,53 @@
             dma((2,)), dma((2,)),
             dma((2, DEPTH)), dma((2, DEPTH)),
             dma((DEPTH,)), dma((DEPTH,)),
-            dma((CHUNKS,)), dma,
+            dma((CHUNKS,)),
         ],
         compiler_params=pltpu.CompilerParams(
             collective_id=1, has_side_effects=True, vmem_limit_bytes=VMEM_BYTES
         ),
         name="layer",
-    )(tokens, w, d_out, rank, index)
+    )(tokens, w, d_out, counts, index)
+
+
+def finish_kernel(attn, d_rows, d_wqkv, index, attn_out, d_tokens, d_wqkv_out):
+    at = pl.program_id(0)
+
+    @pl.when(at == 0)
+    def _():
+        attn_out[...] = attn[...]
+        d_wqkv_out[...] = d_wqkv[...].astype(F32)
+
+    position = lax.broadcasted_iota(jnp.int32, (CHUNK, CAP), 0) + at * CHUNK
+    d_tokens[0] = dot((position == index[...]).astype(BF), d_rows[...]).astype(BF)
+
+
+def finish_call(attn, d_rows, d_wqkv, index, positions):
+    def whole(array):
+        return pl.BlockSpec(array.shape, lambda at: (0,) * array.ndim)
+
+    return pl.pallas_call(
+        finish_kernel,
+        grid=(positions // CHUNK,),
+        out_shape=(
+            jax.ShapeDtypeStruct(attn.shape, BF),
+            jax.ShapeDtypeStruct((1, positions, D), BF),
+            jax.ShapeDtypeStruct(d_wqkv.shape, F32),
+        ),
+        in_specs=[whole(attn), whole(d_rows), whole(d_wqkv), whole(index)],
+        out_specs=(
+            whole(attn),
+            pl.BlockSpec((1, CHUNK, D), lambda at: (0, at, 0)),
+            whole(d_wqkv),
+        ),
+        compiler_params=pltpu.CompilerParams(vmem_limit_bytes=32 * 2**20),
+        name="finish",
+    )(attn, d_rows, d_wqkv, index)
 
 
 def per_device(tokens, w_qkv, vis_index, counts, d_out):
-    extra = (counts[0] - SURE).reshape(SIDE, SIDE).T.reshape(SEQ)
-    order = jnp.arange(SEQ, dtype=jnp.int32)
-    before = jnp.sum(jnp.where(order[None, :] < order[:, None], extra[None, :], 0), axis=1)
-    within = jnp.arange(TAIL, dtype=jnp.int32)
-    rank = jnp.where(within[None, :] < extra[:, None], before[:, None] + within[None, :], -1)
-    rank = rank.reshape(1, SEQ * TAIL).astype(jnp.int32)
-    attn_out, d_tokens, d_wqkv = layer_call(tokens, w_qkv.T, d_out, rank, vis_index)
+    attn, d_rows, d_wqkv = layer_call(tokens, w_qkv.T, d_out, counts, vis_index)
+    attn_out, d_tokens, d_wqkv = finish_call(attn, d_rows, d_wqkv, vis_index, tokens.shape[1])
     return attn_out, d_tokens, d_wqkv.T
 
 

time: 129 us -> 128 us (level)
  local copies, waits for them, and re-layouts: 7.6 us -> 3.15 us
  Pallas kernels: 120 us -> 124 us
    unnamed x5 -> x8, local copies, waits for them, and re-layouts: 6.65 us -> 3.15 us
    pallas_call x0 -> x1, Pallas kernels: none -> 3.43 us  [finish_call(): pl.pallas_call(finish_kernel, grid=(positions // CHUNK,), out_shape=(jax....]
where the time goes in v4:
time: 128 us; the launch traced here: 127 us
  Pallas kernels  124 us (97%)
  local copies, waits for them, and re-layouts  3.15 us (2%)
    pallas_call x1, Pallas kernels, layer_call(): pl.pallas_call(layer_kernel, out_shape=(jax.ShapeDtypeStruct((1, CAP, D),...  120 us
    pallas_call x1, Pallas kernels, finish_call(): pl.pallas_call(finish_kernel, grid=(positions // CHUNK,), out_shape=(jax....  3.43 us
    unnamed x8, local copies, waits for them, and re-layouts  3.15 us

profile of v4, /device:TPU:1, one launch (start us, length us, event | category | flops | bytes accessed | tf_op | source)
XLA Modules:
  0.0 127.3 jit_solution(6849920345715087758)
XLA Ops:
  0.6 0.0 copy-start.3
  0.6 120.1 %layer.1 = (bf16[1,160,1408]{2,1,0:T(8,128)(2,1)}, bf16[160,1408]{1,0:T(8,128)(2,1)}, bf16[264,1408]{1,0:T(8,128)(2,1)}) custom-call(bf16[1,1024,1408]{2,1,0:T(8,128)(2,1)} %tokens_in.1, bf16[264,1408]{1,0:T(8,128)(2,1)} %bitcast.2, bf16[1,160,1408]{2,1,0:T(8,128)(2,1)} %d_out.1, s32[1,16]{1,0:T(1,128)} %counts.1, s32[1,160]{1,0:T(1,128)} %index.3), custom_call_target="tpu_custom_call" | custom-call | tf_op jit(solution)/shard_map/layer/pallas_call | solution.py:598
  120.7 0.0 copy-done.3
  120.7 0.0 copy-start
  120.8 1.1 copy-done
  121.9 0.0 copy-start.1
  121.9 1.0 copy-done.1
  122.9 0.0 copy-start.2
  122.9 1.0 copy-done.2
  123.9 3.4 %finish.1 = (bf16[1,160,1408]{2,1,0:T(8,128)(2,1)}, bf16[1,1024,1408]{2,1,0:T(8,128)(2,1)}, f32[264,1408]{1,0:T(8,128)}) custom-call(bf16[1,160,1408]{2,1,0:T(8,128)(2,1)S(1)} %copy-done.1, bf16[160,1408]{1,0:T(8,128)(2,1)S(1)} %copy-done.2, bf16[264,1408]{1,0:T(8,128)(2,1)S(1)} %copy-done, s32[1,160]{1,0:T(1,128)S(1)} %copy-done.3), custom_call_target="tpu_custom_call" | custom-call | tf_op jit(solution)/shard_map/finish/pallas_call | solution.py:674
Async XLA Ops:
  0.6 120.1 %copy-start.3 = (s32[1,160]{1,0:T(1,128)S(1)}, s32[1,160]{1,0:T(1,128)}, u32[]{:S(2)}) copy-start(s32[1,160]{1,0:T(1,128)} %index.3) | copy-start | bytes 1924
  120.7 1.1 copy-start
  121.9 1.0 copy-start.1
  122.9 1.0 copy-start.2

commit v5 on v4

--- a/solution.py
+++ b/solution.py
@@ -419,13 +419,6 @@
             att_send[:, :HALF, :] = att[:FIRST].reshape(SEQ, HALF, LANES)
             a_start(0)
 
-        @pl.when(at == LIVE // QB - 1)
-        def _():
-            for axis in (0, 1):
-                for sign in (1, -1):
-                    w_onward(axis, sign, 2).wait_recv()
-                    w_across(axis, sign, True).start()
-
     attend(q, kt, k, v, vt, g, att, dq, dkt, dvt, between)
 
     dk = (dkt[...].T * LN2).astype(BF)
@@ -449,6 +442,10 @@
     for step in (2, 1, 3):
         for axis in (0, 1):
             d_copy(axis, step).start()
+    for axis in (0, 1):
+        for sign in (1, -1):
+            w_onward(axis, sign, 2).wait_recv()
+            w_across(axis, sign, True).start()
     for axis in (0, 1):
         d_recv[axis, place[axis]] = d_send[axis, place[axis]]
 
@@ -514,16 +511,6 @@
     for axis in (0, 1):
         part_recv[axis, place[axis]] = part_send[axis, place[axis]]
 
-    def a_wait(step, carry):
-        for half in (0, 1):
-            a_copy(half, step).wait_send()
-            a_arrival(half, step).wait_recv()
-        return carry
-
-    lax.fori_loop(1, SEQ, a_wait, 0)
-    for head in range(HEADS):
-        attn_out[0, :, head * HEAD:(head + 1) * HEAD] = att_recv[head, :, :HEAD]
-
     for step in range(1, DEPTH):
         z_arrival(0, step).wait_recv()
     total = z_recv[0].astype(F32)
@@ -538,6 +525,16 @@
         return remote(z_all.at[slot], z_other.at[slot], (o_ssem, o_rsem), step, other, "batch")
 
     o_copy(0).start()
+
+    def a_wait(step, carry):
+        for half in (0, 1):
+            a_copy(half, step).wait_send()
+            a_arrival(half, step).wait_recv()
+        return carry
+
+    lax.fori_loop(1, SEQ, a_wait, 0)
+    for head in range(HEADS):
+        attn_out[0, :, head * HEAD:(head + 1) * HEAD] = att_recv[head, :, :HEAD]
 
     for axis in (0, 1):
         for step in (1, 2, 3):
@@ -685,7 +682,7 @@
             pl.BlockSpec((1, CHUNK, D), lambda at: (0, at, 0)),
             whole(d_wqkv),
         ),
-        compiler_params=pltpu.CompilerParams(vmem_limit_bytes=32 * 2**20),
+        compiler_params=pltpu.CompilerParams(vmem_limit_bytes=VMEM_BYTES),
         name="finish",
     )(attn, d_rows, d_wqkv, index)
 

time: 128 us -> 125 us (0.977)
  local copies, waits for them, and re-layouts: 3.15 us -> 0 us
    unnamed x8 -> x0, local copies, waits for them, and re-layouts: 3.15 us -> none
    pallas_call x1, Pallas kernels: 3.43 us -> 4.86 us  [finish_call(): pl.pallas_call(finish_kernel, grid=(positions // CHUNK,), out_shape=(jax....]
where the time goes in v5:
time: 125 us
  Pallas kernels  124 us (99%)
    pallas_call x1, Pallas kernels, layer_call(): pl.pallas_call(layer_kernel, out_shape=(jax.ShapeDtypeStruct((1, CAP, D),...  119 us
    pallas_call x1, Pallas kernels, finish_call(): pl.pallas_call(finish_kernel, grid=(positions // CHUNK,), out_shape=(jax....  4.86 us

profile of v5, /device:TPU:1, one launch (start us, length us, event | category | flops | bytes accessed | tf_op | source)
XLA Modules:
  0.0 124.7 jit_solution(1105094714576829550)
XLA Ops:
  0.6 119.2 %layer.1 = (bf16[1,160,1408]{2,1,0:T(8,128)(2,1)}, bf16[160,1408]{1,0:T(8,128)(2,1)}, bf16[264,1408]{1,0:T(8,128)(2,1)}) custom-call(bf16[1,1024,1408]{2,1,0:T(8,128)(2,1)} %tokens_in.1, bf16[264,1408]{1,0:T(8,128)(2,1)} %bitcast.2, bf16[1,160,1408]{2,1,0:T(8,128)(2,1)} %d_out.1, s32[1,16]{1,0:T(1,128)} %counts.1, s32[1,160]{1,0:T(1,128)} %index.3), custom_call_target="tpu_custom_call" | custom-call | tf_op jit(solution)/shard_map/layer/pallas_call | solution.py:595
  119.9 4.9 %finish.1 = (bf16[1,160,1408]{2,1,0:T(8,128)(2,1)}, bf16[1,1024,1408]{2,1,0:T(8,128)(2,1)}, f32[264,1408]{1,0:T(8,128)}) custom-call(bf16[1,160,1408]{2,1,0:T(8,128)(2,1)} %get-tuple-element.9.attn, bf16[160,1408]{1,0:T(8,128)(2,1)} %get-tuple-element.10.d_rows, bf16[264,1408]{1,0:T(8,128)(2,1)} %get-tuple-element.11.d_wqkv, s32[1,160]{1,0:T(1,128)} %index.3), custom_call_target="tpu_custom_call" | custom-call | tf_op jit(solution)/shard_map/finish/pallas_call | solution.py:671
